TPU v7x, 256 devices: a whole 4x4x8 slice. The times are simulated.
256 devices in a mesh: ia: 8 (over y, core), wa: 8 (over x, z_hi), ao: 4 (over z_lo).
Axes of the slice: x: 4, y: 4, z: 8 (z_hi: 2, z_lo: 4; z = z_hi * 4 + z_lo), core: 2. Of those that a mesh axis runs over, the one named last changes fastest.
Arguments:
- residual: bfloat16 [2048, 14848], P(('ia', 'wa'), 'ao'), may hold values from -6 to 6
- context: bfloat16 [2048, 14848], P('ia', 'wa'), may hold values from -6 to 6
- proj_weight: bfloat16 [8, 1856, 14848], P('wa', 'ia', 'ao'), may hold values from -0.046875 to 0.046875
- out_grad: bfloat16 [2048, 14848], P(('ia', 'wa'), 'ao'), may hold values from -4 to 4
Outputs:
- updated: bfloat16 [2048, 14848], P(('ia', 'wa'), 'ao')
- context_grad: bfloat16 [2048, 14848], P(('ia', 'ao'), 'wa')
- weight_grad: bfloat16 [8, 1856, 14848], P('wa', 'ia', 'ao')
All inputs are finite; a program needn't handle non-finite values.
Results may differ from a plain program's by a relative error of at most 0.017.
Values may be sent and summed in bfloat16 or wider, within the bound.
A program may use at most 128 MiB of HBM per device.

v0:
```python
import jax
import jax.numpy as jnp
from jax import lax
from jax.sharding import PartitionSpec as P


def per_device(residual, context, proj_weight, out_grad):
    weight = lax.all_gather(proj_weight, "ia", axis=1, tiled=True)[0]
    subset = context
    projected = lax.psum_scatter(
        jnp.dot(subset, weight, preferred_element_type=jnp.float32).astype(jnp.bfloat16),
        "wa",
        scatter_dimension=0,
        tiled=True,
    ).astype(jnp.float32)
    updated = (residual.astype(jnp.float32) + projected).astype(jnp.bfloat16)
    grad_rows = lax.all_gather(out_grad, "wa", axis=0, tiled=True)
    subset = grad_rows
    context_grad = lax.psum_scatter(
        lax.dot_general(
            subset, weight, (((1,), (1,)), ((), ())), preferred_element_type=jnp.float32
        ).astype(jnp.bfloat16),
        "ao",
        scatter_dimension=0,
        tiled=True,
    )
    subset = context
    summed = lax.psum_scatter(
        lax.dot_general(
            subset, grad_rows, (((0,), (0,)), ((), ())), preferred_element_type=jnp.float32
        ).astype(jnp.bfloat16),
        "ia",
        scatter_dimension=0,
        tiled=True,
    )
    weight_grad = summed[None]
    return (updated, context_grad, weight_grad)


def solution(mesh):
    in_specs = (P(("ia", "wa"), "ao"), P("ia", "wa"), P("wa", "ia", "ao"), P(("ia", "wa"), "ao"))
    out_specs = (P(("ia", "wa"), "ao"), P(("ia", "ao"), "wa"), P("wa", "ia", "ao"))
    return jax.shard_map(
        per_device, mesh=mesh, in_specs=in_specs, out_specs=out_specs, check_vma=False
    )
```

profile of v0, /device:TPU:65, one launch (start us, length us, event | category | flops | bytes accessed | tf_op | source)
XLA Modules:
  0.0 377.0 jit_solution(3805056148399148322)
XLA Ops:
  7.2 0.0 copy-start
  7.2 0.0 all-gather.3.cloned.1.call-start
  7.2 0.7 all-gather.3.cloned.1.call-update
  7.9 0.0 all-gather.5.cloned.1.call-start
  8.0 0.7 all-gather.5.cloned.1.call-update
  8.7 0.0 reduce-scatter.6.cloned.1.call-start
  8.7 78.8 %all-gather.3.cloned.1.call-done = bf16[1,1856,3712]{2,1,0:T(8,128)(2,1)} async-done(((bf16[1,232,3712]{2,1,0:T(8,128)(2,1)}), bf16[1,1856,3712]{2,1,0:T(8,128)(2,1)}) %all-gather.3.cloned.1.call-update) | async-done | bytes 13778960 | tf_op jit(solution)/shard_map/all_gather | solution.py:8
  87.5 0.0 copy-done
  87.5 10.4 %fusion.4 = bf16[256,3712]{1,0:T(8,128)(2,1)} fusion(bf16[256,1856]{0,1:T(8,128)(2,1)S(1)} %copy-done, bf16[1,1856,3712]{2,1,0:T(8,128)(2,1)} %all-gather.3.cloned.1.call-done), kind=kOutput, calls=%fused_computation.5 | convolution fusion | flops 3528359936 | bytes 16629760 | tf_op jit(solution)/shard_map/dot_general | solution.py:11
  97.9 0.0 reduce-scatter.6.cloned.1.call-update
  97.9 0.0 reduce-scatter.8.cloned.1.call-start
  98.0 62.2 %all-gather.5.cloned.1.call-done = bf16[256,3712]{1,0:T(8,128)(2,1)} async-done(((bf16[32,3712]{1,0:T(8,128)(2,1)}), bf16[256,3712]{1,0:T(8,128)(2,1)}) %all-gather.5.cloned.1.call-update) | async-done | bytes 1900560 | tf_op jit(solution)/shard_map/all_gather | solution.py:17
  160.2 0.0 copy-start.1
  160.2 10.8 %fusion.7 = bf16[256,1856]{1,0:T(8,128)(2,1)} fusion(bf16[256,3712]{1,0:T(8,128)(2,1)} %all-gather.5.cloned.1.call-done, bf16[1,1856,3712]{2,1,0:T(8,128)(2,1)} %all-gather.3.cloned.1.call-done), kind=kOutput, calls=%fused_computation.6 | convolution fusion | flops 3527884800 | bytes 16629760 | tf_op jit(solution)/shard_map/dot_general | solution.py:20
  171.0 0.0 reduce-scatter.8.cloned.1.call-update
  171.0 0.0 reduce-scatter.10.cloned.1.call-start
  171.1 0.0 copy-done.1
  171.1 7.1 %convolution_convert_fusion = bf16[1856,3712]{1,0:T(8,128)(2,1)} fusion(bf16[256,1856]{0,1:T(8,128)(2,1)S(1)} %copy-done, bf16[256,3712]{1,0:T(8,128)(2,1)S(1)} %copy-done.1), kind=kOutput, calls=%fused_computation | convolution fusion | flops 3534299136 | bytes 16629760 | tf_op jit(solution)/shard_map/dot_general | solution.py:29
  178.1 0.0 copy-start.2
  178.1 0.0 reduce-scatter.10.cloned.1.call-update
  178.2 75.5 %reduce-scatter.6.cloned.1.call-done = bf16[32,3712]{1,0:T(8,128)(2,1)} async-done(((bf16[256,3712]{1,0:T(8,128)(2,1)}), bf16[32,3712]{1,0:T(8,128)(2,1)}) %reduce-scatter.6.cloned.1.call-update) | async-done | bytes 237584 | tf_op jit(solution)/shard_map/reduce_scatter | solution.py:10
  253.6 0.0 copy-done.2
  253.6 1.7 add_convert_fusion
  255.3 30.3 %reduce-scatter.8.cloned.1.call-done = bf16[64,1856]{1,0:T(8,128)(2,1)} async-done(((bf16[256,1856]{1,0:T(8,128)(2,1)}), bf16[64,1856]{1,0:T(8,128)(2,1)}) %reduce-scatter.8.cloned.1.call-update) | async-done | bytes 237584 | tf_op jit(solution)/shard_map/reduce_scatter | solution.py:19
  285.6 84.9 %reduce-scatter.10.cloned.1.call-done = bf16[232,3712]{1,0:T(8,128)(2,1)} async-done(((bf16[1856,3712]{1,0:T(8,128)(2,1)}), bf16[232,3712]{1,0:T(8,128)(2,1)}) %reduce-scatter.10.cloned.1.call-update) | async-done | bytes 1722384
Async XLA Ops:
  7.2 80.4 %copy-start = (bf16[256,1856]{0,1:T(8,128)(2,1)S(1)}, bf16[256,1856]{0,1:T(8,128)(2,1)}, u32[]{:S(2)}) copy-start(bf16[256,1856]{0,1:T(8,128)(2,1)} %param.5) | copy-start | bytes 2850820
  7.2 80.3 %all-gather.3.cloned.1.call-start = ((), (), s32[]{:S(2)}) async-start(), calls=%async_computation.3 | async-start | bytes 15501312 | tf_op jit(solution)/shard_map/all_gather | solution.py:8
  7.9 152.2 %all-gather.5.cloned.1.call-start = ((), (), s32[]{:S(2)}) async-start(), calls=%async_computation.5 | async-start | bytes 2138112 | tf_op jit(solution)/shard_map/all_gather | solution.py:17
  8.7 244.9 %reduce-scatter.6.cloned.1.call-start = ((), (), s32[]{:S(2)}) async-start(), calls=%async_computation.4 | async-start | bytes 2138112 | tf_op jit(solution)/shard_map/reduce_scatter | solution.py:10
  97.9 187.7 %reduce-scatter.8.cloned.1.call-start = ((), (), s32[]{:S(2)}) async-start(), calls=%async_computation.6 | async-start | bytes 1228800 | tf_op jit(solution)/shard_map/reduce_scatter | solution.py:19
  160.2 10.9 %copy-start.1 = (bf16[256,3712]{1,0:T(8,128)(2,1)S(1)}, bf16[256,3712]{1,0:T(8,128)(2,1)}, u32[]{:S(2)}) copy-start(bf16[256,3712]{1,0:T(8,128)(2,1)} %all-gather.5.cloned.1.call-done) | copy-start | bytes 5701636
  171.0 199.5 %reduce-scatter.10.cloned.1.call-start = ((), (), s32[]{:S(2)}) async-start(), calls=%async_computation.7 | async-start | bytes 15501312
  178.1 75.5 %copy-start.2 = (bf16[32,3712]{1,0:T(8,128)(2,1)S(1)}, bf16[32,3712]{1,0:T(8,128)(2,1)}, u32[]{:S(2)}) copy-start(bf16[32,3712]{1,0:T(8,128)(2,1)} %param.4) | copy-start | bytes 712708
Sparse Core Ops, SparseCore 0:
  9.9 77.5 all-gather.2
  90.1 69.9 all-gather.4
  164.3 89.3 reduce-scatter.5
  256.6 28.9 reduce-scatter.7
  288.8 81.6 reduce-scatter.9
where the time goes:
time: 379 us; the launch traced here: 377 us
  waiting for transfers between devices  333 us (88%)
  matrix products  28.2 us (7%)
  between operations  13.8 us (4%)
    unnamed x6, waiting for transfers between devices  86.3 us
    all_gather x1, waiting for transfers between devices, per_device(): weight = lax.all_gather(proj_weight, 'ia', axis=1, tiled=True)[0]  78.8 us
    reduce_scatter x1, waiting for transfers between devices, per_device(): lax.psum_scatter(jnp.dot(subset, weight, preferred_element_type=jnp.float...  75.5 us
    all_gather x1, waiting for transfers between devices, per_device(): grad_rows = lax.all_gather(out_grad, 'wa', axis=0, tiled=True)  62.2 us
    reduce_scatter x1, waiting for transfers between devices, per_device(): lax.psum_scatter(lax.dot_general(subset, weight, (((1,), (1,)), ((), ()))...  30.3 us
    dot_general x1, matrix products, per_device(): lax.dot_general(subset, weight, (((1,), (1,)), ((), ())), preferred_eleme...  10.8 us
    dot_general x1, matrix products, per_device(): jnp.dot(subset, weight, preferred_element_type=jnp.float32)  10.4 us
  transfers between devices with their start and end apart: 5, of which 5 were waited for; matrix products, arithmetic and copies ran while one was open for 8% of the time, Pallas kernels for 0%

commit v1 on v0

v1 whole, which is shorter than its diff:
```python
import jax
import jax.numpy as jnp
from jax import lax
from jax.experimental import pallas as pl
from jax.experimental.pallas import tpu as pltpu
from jax.sharding import PartitionSpec as P

MESH = pl.DeviceIdType.MESH
BF16 = jnp.bfloat16
F32 = jnp.float32

ROWS = 232
D_ROW = 3712
SHIFT = 1792
WIN = 1920
NC = 3
CW = WIN // NC
TOK = 32


class Sems:
    def __init__(self):
        self.n = 0

    def take(self, count):
        base = self.n
        self.n += count
        return base


N_SEMS = 160


def kernel(
    res_ref, ctx_ref, w_ref, g_ref,
    upd_ref, cg_ref, wg_ref,
    Wb, Gb, Xs, Xb, XT,
    bufA, RA, bufB1, bufB2, RB1, RB2, PB1, PB2, PX, accP,
    bufY, RY, bufZ, RZ, bufC, RC, own,
    OWN, DY, RDY, RDC, TZ, RDZ,
    DWs, RW,
    ss, rs, ls,
):
    ia = lax.axis_index("ia")
    wa = lax.axis_index("wa")
    zl = lax.axis_index("ao")
    y, c = lax.div(ia, 2), lax.rem(ia, 2)
    x, zh = lax.div(wa, 2), lax.rem(wa, 2)
    oc, zn = 1 - c, 1 - zh

    def flip(v):
        return v + 1 - 2 * lax.rem(v, 2)

    ya, yb = flip(y), 3 - y

    def w_pair(yy, cc):
        return (1 - cc) * flip(yy) + cc * (3 - yy)

    def t_pair(yy, cc):
        return cc * flip(yy) + (1 - cc) * (3 - yy)

    wp, tp = w_pair(y, c), t_pair(y, c)
    xp, xm, x2 = lax.rem(x + 1, 4), lax.rem(x + 3, 4), lax.rem(x + 2, 4)

    def dev(yy=y, cc=c, xx=x, hh=zh, ll=zl):
        return (2 * yy + cc, 2 * xx + hh, ll)

    other_core = dev(cc=oc)
    partners = [
        other_core,
        dev(yy=ya, cc=0), dev(yy=ya, cc=1), dev(yy=yb, cc=0), dev(yy=yb, cc=1),
        dev(xx=xp), dev(xx=xm),
        dev(hh=zn), dev(hh=zn, cc=oc),
    ] + [dev(ll=lax.rem(zl + m, 4)) for m in (1, 2, 3)]

    barrier = pltpu.get_barrier_semaphore()
    for p in partners:
        pl.semaphore_signal(barrier, inc=1, device_id=p, device_id_type=MESH)
    pl.semaphore_wait(barrier, len(partners))

    s_idx, r_idx, l_idx = Sems(), Sems(), Sems()
    sent = []

    def send(src, dst, r, to, s=None):
        if s is None:
            s = s_idx.take(1)
        cp = pltpu.make_async_remote_copy(
            src_ref=src, dst_ref=dst, send_sem=ss.at[s], recv_sem=rs.at[r],
            device_id=to, device_id_type=MESH,
        )
        cp.start()
        return cp

    def post(*args):
        sent.append(send(*args))

    def got(dst, r):
        pltpu.make_async_remote_copy(
            src_ref=dst, dst_ref=dst, send_sem=ss.at[0], recv_sem=rs.at[r],
            device_id=other_core, device_id_type=MESH,
        ).wait_recv()

    def local(src, dst):
        cp = pltpu.make_async_copy(src, dst, ls.at[l_idx.take(1)])
        cp.start()
        return cp

    def window(cc):
        return pl.ds(pl.multiple_of(cc * SHIFT, 128), WIN)

    r_g0 = r_idx.take(2)
    r_g1 = r_idx.take(2)
    g_own = g_ref.at[:, window(c)]
    g_oth = g_ref.at[:, window(oc)]
    g_local = local(g_own, Gb.at[0, c, x, zh])
    post(g_oth, Gb.at[0, c, x, zh], r_g0 + c, other_core)
    post(g_own, Gb.at[0, c, x, zh], r_g1 + c, dev(hh=zn))
    post(g_oth, Gb.at[0, c, x, zh], r_g1 + c, dev(hh=zn, cc=oc))

    r_w = r_idx.take(4 * NC)

    def w_cols(cc, j):
        return pl.ds(pl.multiple_of(cc * SHIFT + j * CW, 128), CW)

    w_locals = []
    for j in range(NC):
        cols = pl.ds(j * CW, CW)
        w_locals.append(local(w_ref.at[:, w_cols(c, j)], Wb.at[c, :, cols]))
        post(w_ref.at[:, w_cols(oc, j)], Wb.at[c, :, cols], r_w + c * NC + j, other_core)

    def send_w(j):
        cols = pl.ds(j * CW, CW)
        for cc, yy in ((0, ya), (1, yb)):
            post(w_ref.at[:, w_cols(cc, j)], Wb.at[2 + c, :, cols],
                 r_w + (2 + c) * NC + j, dev(yy=yy, cc=cc))

    r_y = r_idx.take(2)
    r_xp = r_idx.take(4)
    r_xm = r_idx.take(4)
    r_f = r_idx.take(4)

    def unit(p, xx, h):
        return Gb.at[p, :, xx, h]

    def to_x(p, k, h):
        post(unit(p, x, h), unit(p, x, h), r_xp + 2 * p + k, dev(xx=xp))
        post(unit(p, x, h), unit(p, x, h), r_xm + 2 * p + k, dev(xx=xm))

    def forward(k, h):
        got(unit(0, xm, h), r_xp + k)
        post(unit(0, xm, h), unit(0, xm, h), r_f + k, dev(xx=xp))
        got(unit(1, xp, h), r_xm + 2 + k)
        post(unit(1, xp, h), unit(1, xp, h), r_f + 2 + k, dev(xx=xm))

    g_local.wait()
    got(Gb.at[0, oc, x, zh], r_g0 + oc)
    post(unit(0, x, zh), unit(1, x, zh), r_y, dev(yy=tp))
    to_x(0, 0, zh)
    send_w(0)

    for g in range(8):
        piece = ctx_ref[:, g * ROWS:(g + 1) * ROWS]
        piece = jnp.concatenate([piece, jnp.zeros((256, 256 - ROWS), BF16)], axis=1)
        Xs[g] = piece.reshape(4, 64, 256)
    r_c = r_idx.take(8)

    x_locals = []
    for q, yy in enumerate((y, w_pair(y, c))):
        x_locals.append(local(Xs.at[pl.ds(2 * yy, 2)], Xb.at[pl.ds(2 * q, 2), c]))
    for q, yy in enumerate((y, w_pair(y, oc))):
        post(Xs.at[pl.ds(2 * yy, 2)], Xb.at[pl.ds(2 * q, 2), c], r_c + 2 * c + q, other_core)
    for y_to, cc in ((yb, 0), (ya, 1)):
        for q, yy in enumerate((y_to, w_pair(y_to, cc))):
            post(Xs.at[pl.ds(2 * yy, 2)], Xb.at[pl.ds(2 * q, 2), 2 + c],
                 r_c + 2 * (2 + c) + q, dev(yy=y_to, cc=cc))

    got(unit(1, x, zh), r_y)
    to_x(1, 0, zh)
    forward(0, zh)

    def got_x(blk):
        for q in range(2):
            got(Xb.at[pl.ds(2 * q, 2), blk], r_c + 2 * blk + q)

    def transpose_x(blk):
        for s in range(4):
            t = Xb[s, blk].reshape(256, 256)
            XT[s, :, blk * 256:(blk + 1) * 256] = t.T

    for cp in x_locals:
        cp.wait()
    got_x(oc)
    transpose_x(0)
    transpose_x(1)

    for core in range(2):
        got(Gb.at[0, core, x, zn], r_g1 + core)
    post(unit(0, x, zn), unit(1, x, zn), r_y + 1, dev(yy=tp))
    to_x(0, 1, zn)
    for j in range(1, NC):
        send_w(j)
    got(unit(1, x, zn), r_y + 1)
    to_x(1, 1, zn)
    forward(1, zn)

    for blk in (2, 3):
        got_x(blk)
        transpose_x(blk)

    for cp in w_locals:
        cp.wait()
    for j in range(NC):
        cols = pl.ds(j * CW, CW)
        got(Wb.at[oc, :, cols], r_w + oc * NC + j)
        for s in (2, 3):
            got(Wb.at[s, :, cols], r_w + s * NC + j)
    keep = (c == 0).astype(BF16)
    for s in range(4):
        Wb[s, :, 0:128] = Wb[s, :, 0:128] * keep

    def cols_of(j):
        return pl.ds(pl.multiple_of(j * CW, 128), CW)

    def project(d, j):
        total = None
        for s in range(4):
            a = Xb[s, :, d].reshape(256, 256)[:, :ROWS]
            part = jnp.dot(a, Wb[s, :, cols_of(j)], preferred_element_type=F32)
            total = part if total is None else total + part
        return total.reshape(2, 128, CW)

    r_a = r_idx.take(2 * NC)
    r_b1 = r_idx.take(2 * NC)
    r_b2 = r_idx.take(2 * NC)
    s_a, s_b1, s_b2 = s_idx.take(2 * NC), s_idx.take(2 * NC), s_idx.take(2 * NC)
    to_xp, to_xm = dev(xx=xp), dev(xx=xm)

    def drain(src, s):
        pltpu.make_async_remote_copy(
            src_ref=src, dst_ref=src, send_sem=ss.at[s], recv_sem=rs.at[0],
            device_id=other_core, device_id_type=MESH,
        ).wait_send()

    @pl.loop(0, NC)
    def _(j):
        bufA[j] = project(x2, j).astype(BF16)
        send(bufA.at[j, 0], RA.at[j, 0], r_a + 2 * j, to_xp, s_a + 2 * j)
        send(bufA.at[j, 1], RA.at[j, 1], r_a + 2 * j + 1, to_xm, s_a + 2 * j + 1)

    r_dy, r_dc, r_dz = r_idx.take(4), r_idx.take(16), r_idx.take(4)
    s_dz = s_idx.take(4)
    blocks = (x, xp, xm, x2)

    def back(k):
        d = blocks[k]

        @pl.loop(0, 4)
        def _(s):
            g = Gb[:, :, d].reshape(256, WIN)
            t = lax.dot_general(g, Wb[s], (((1,), (1,)), ((), ())),
                                preferred_element_type=F32).astype(BF16)
            t = jnp.concatenate([t, jnp.zeros((256, 256 - ROWS), BF16)], axis=1)
            t = t.reshape(2, 2, 64, 256)
            OWN[k, s] = t[0]
            DY[k, s] = t[1]

        post(DY.at[k], RDY.at[k], r_dy + k, dev(yy=tp))

    back(0)
    for h, k in ((zh, 0), (zn, 1)):
        got(unit(1, xm, h), r_xp + 2 + k)
        got(unit(0, xp, h), r_xm + k)
    back(1)
    back(2)

    @pl.loop(0, NC)
    def _(j):
        v = project(xp, j)
        bufB1[j, 1] = v[1].astype(BF16)
        send(bufB1.at[j, 1], RB1.at[j, 1], r_b1 + 2 * j + 1, to_xp, s_b1 + 2 * j + 1)
        PB1[j] = v[0]
        v = project(xm, j)
        bufB2[j, 0] = v[0].astype(BF16)
        send(bufB2.at[j, 0], RB2.at[j, 0], r_b2 + 2 * j, to_xm, s_b2 + 2 * j)
        PB2[j] = v[1]

    for k, h in ((0, zh), (1, zn)):
        got(unit(0, x2, h), r_f + k)
        got(unit(1, x2, h), r_f + 2 + k)
    back(3)

    r_wg = r_idx.take(4 * NC)
    s_wg = s_idx.take(3 * NC)

    def grad(s, j):
        a = XT[s]
        b = Gb[:, :, :, :, :, cols_of(j)].reshape(1024, CW)
        return jnp.dot(a, b, preferred_element_type=F32)[:ROWS].astype(BF16)

    for core in range(2):
        to = dev(yy=wp, cc=core)

        @pl.loop(0, NC)
        def _(j):
            DWs[core, j] = grad(2 + core, j)
            send(DWs.at[core, j], RW.at[c, 1, j], r_wg + (2 * c + 1) * NC + j, to, s_wg + core * NC + j)

    @pl.loop(0, NC)
    def _(j):
        got(RA.at[j, 0], r_a + 2 * j)
        bufB1[j, 0] = (PB1[j] + RA[j, 0].astype(F32)).astype(BF16)
        send(bufB1.at[j, 0], RB1.at[j, 0], r_b1 + 2 * j, to_xp, s_b1 + 2 * j)
        got(RA.at[j, 1], r_a + 2 * j + 1)
        bufB2[j, 1] = (PB2[j] + RA[j, 1].astype(F32)).astype(BF16)
        send(bufB2.at[j, 1], RB2.at[j, 1], r_b2 + 2 * j + 1, to_xm, s_b2 + 2 * j + 1)

    own_groups = (y, wp)
    got_groups = (tp, w_pair(tp, c))
    for k in range(4):
        got(RDY.at[k], r_dy + k)
        for q in range(2):
            for part, group in ((OWN, own_groups[q]), (RDY, got_groups[q])):
                post(part.at[k, pl.ds(2 * q, 2), oc], RDC.at[k, group],
                     r_dc + 4 * k + group, other_core)

    @pl.loop(0, NC)
    def _(j):
        DWs[2, j] = grad(oc, j)
        send(DWs.at[2, j], RW.at[c, 0, j], r_wg + 2 * c * NC + j, other_core, s_wg + 2 * NC + j)

    @pl.loop(0, NC)
    def _(j):
        RW[c, 0, j] = grad(c, j)

    for k in range(4):
        d = blocks[k]
        for group in range(4):
            got(RDC.at[k, group], r_dc + 4 * k + group)
        for q in range(2):
            for part, group in ((OWN, own_groups[q]), (RDY, got_groups[q])):
                TZ[k, group] = (part[k, 2 * q:2 * q + 2, c].astype(F32)
                                + RDC[k, group].astype(F32)).astype(BF16)

        @pl.when(d != zl)
        def _():
            send(TZ.at[k], RDZ.at[zl], r_dz + zl, dev(ll=d), s_dz + k)

        @pl.when(d == zl)
        def _():
            RDZ[zl] = TZ[k]

    r_py, r_pz, r_pc = r_idx.take(NC), r_idx.take(NC), r_idx.take(NC)
    s_py, s_pz, s_pc = s_idx.take(NC), s_idx.take(NC), s_idx.take(NC)

    @pl.loop(0, NC)
    def _(j):
        PX[j] = project(x, j)

    @pl.loop(0, NC)
    def _(j):
        got(RB1.at[j, 1], r_b1 + 2 * j + 1)
        got(RB2.at[j, 1], r_b2 + 2 * j + 1)
        bufY[j] = (PX[j, 1] + RB1[j, 1].astype(F32) + RB2[j, 1].astype(F32)).astype(BF16)
        send(bufY.at[j], RY.at[j], r_py + j, dev(yy=tp), s_py + j)

    @pl.loop(0, NC)
    def _(j):
        got(RB1.at[j, 0], r_b1 + 2 * j)
        got(RB2.at[j, 0], r_b2 + 2 * j)
        v = PX[j, 0] + RB1[j, 0].astype(F32) + RB2[j, 0].astype(F32)
        got(RY.at[j], r_py + j)
        v = v + RY[j].astype(F32)
        accP[j] = v.reshape(2, 2, TOK, CW)
        bufZ[j] = accP[j, :, zn].astype(BF16)
        send(bufZ.at[j], RZ.at[j], r_pz + j, dev(hh=zn), s_pz + j)

    for m in (1, 2, 3):
        src = lax.rem(zl + m, 4)
        got(RDZ.at[src], r_dz + src)
    total = RDZ[0].astype(F32)
    for m in (1, 2, 3):
        total = total + RDZ[m].astype(F32)
    cg_ref[...] = total.astype(BF16).reshape(8, 64, 256)

    @pl.loop(0, NC)
    def _(j):
        got(RZ.at[j], r_pz + j)
        own[j] = accP[j, c, zh] + RZ[j, c].astype(F32)
        bufC[j] = accP[j, oc, zh] + RZ[j, oc].astype(F32)
        send(bufC.at[j], RC.at[j], r_pc + j, other_core, s_pc + j)

    @pl.loop(0, NC)
    def _(j):
        got(RW.at[oc, 0, j], r_wg + 2 * oc * NC + j)
        for w in range(2):
            got(RW.at[w, 1, j], r_wg + (2 * w + 1) * NC + j)

    for w in range(2):
        @pl.loop(0, NC)
        def _(j):
            cols = pl.ds(pl.multiple_of(w * SHIFT + j * CW, 128), CW)
            wg_ref[:, cols] = (RW[w, 0, j].astype(F32) + RW[w, 1, j].astype(F32)).astype(BF16)

    for j in range(NC):
        got(RC.at[j], r_pc + j)
    for w in (1, 0):
        for j in range(NC):
            cols = slice(w * SHIFT + j * CW, w * SHIFT + (j + 1) * CW)
            v = jnp.where(c == w, own[j], RC[j])
            upd_ref[:, cols] = (res_ref[:, cols].astype(F32) + v).astype(BF16)

    for cp in sent:
        cp.wait_send()
    for j in range(NC):
        for h in range(2):
            drain(bufA.at[j, h], s_a + 2 * j + h)
            drain(bufB1.at[j, h], s_b1 + 2 * j + h)
            drain(bufB2.at[j, h], s_b2 + 2 * j + h)
        for s in range(3):
            drain(DWs.at[s, j], s_wg + s * NC + j)
        drain(bufY.at[j], s_py + j)
        drain(bufZ.at[j], s_pz + j)
        drain(bufC.at[j], s_pc + j)
    for k in range(4):
        @pl.when(blocks[k] != zl)
        def _():
            drain(TZ.at[k], s_dz + k)


def per_device(residual, context, proj_weight, out_grad):
    vmem = pl.BlockSpec(memory_space=pltpu.VMEM)
    anywhere = pl.BlockSpec(memory_space=pl.ANY)
    shape = jax.ShapeDtypeStruct
    updated, context_grad, weight_grad = pl.pallas_call(
        kernel,
        out_shape=(
            shape((TOK, D_ROW), BF16),
            shape((8, 64, 256), BF16),
            shape((ROWS, D_ROW), BF16),
        ),
        in_specs=[vmem, vmem, anywhere, anywhere],
        out_specs=(vmem, vmem, vmem),
        scratch_shapes=[
            pltpu.VMEM((4, ROWS, WIN), BF16),
            pltpu.VMEM((2, 2, 4, 2, TOK, WIN), BF16),
            pltpu.VMEM((8, 4, 64, 256), BF16),
            pltpu.VMEM((4, 4, 4, 64, 256), BF16),
            pltpu.VMEM((4, 256, 1024), BF16),
            pltpu.VMEM((NC, 2, 128, CW), BF16),
            pltpu.VMEM((NC, 2, 128, CW), BF16),
            pltpu.VMEM((NC, 2, 128, CW), BF16),
            pltpu.VMEM((NC, 2, 128, CW), BF16),
            pltpu.VMEM((NC, 2, 128, CW), BF16),
            pltpu.VMEM((NC, 2, 128, CW), BF16),
            pltpu.VMEM((NC, 128, CW), F32),
            pltpu.VMEM((NC, 128, CW), F32),
            pltpu.VMEM((NC, 2, 128, CW), F32),
            pltpu.VMEM((NC, 2, 2, TOK, CW), F32),
            pltpu.VMEM((NC, 128, CW), BF16),
            pltpu.VMEM((NC, 128, CW), BF16),
            pltpu.VMEM((NC, 2, TOK, CW), BF16),
            pltpu.VMEM((NC, 2, TOK, CW), BF16),
            pltpu.VMEM((NC, TOK, CW), F32),
            pltpu.VMEM((NC, TOK, CW), F32),
            pltpu.VMEM((NC, TOK, CW), F32),
            pltpu.VMEM((4, 4, 2, 64, 256), BF16),
            pltpu.VMEM((4, 4, 2, 64, 256), BF16),
            pltpu.VMEM((4, 4, 2, 64, 256), BF16),
            pltpu.VMEM((4, 4, 2, 64, 256), BF16),
            pltpu.VMEM((4, 4, 2, 64, 256), BF16),
            pltpu.VMEM((4, 4, 2, 64, 256), BF16),
            pltpu.VMEM((3, NC, ROWS, CW), BF16),
            pltpu.VMEM((2, 2, NC, ROWS, CW), BF16),
            pltpu.SemaphoreType.DMA((N_SEMS,)),
            pltpu.SemaphoreType.DMA((N_SEMS,)),
            pltpu.SemaphoreType.DMA((16,)),
        ],
        compiler_params=pltpu.CompilerParams(
            collective_id=0, has_side_effects=True, vmem_limit_bytes=60 * 2**20
        ),
        cost_estimate=pl.CostEstimate(
            flops=6 * 1024 * 928 * WIN, bytes_accessed=8 * 2**20, transcendentals=0
        ),
    )(residual, context, proj_weight[0], out_grad)
    context_grad = context_grad[:, :, :ROWS].transpose(1, 0, 2).reshape(64, 8 * ROWS)
    return updated, context_grad, weight_grad[None]


def solution(mesh):
    in_specs = (P(("ia", "wa"), "ao"), P("ia", "wa"), P("wa", "ia", "ao"), P(("ia", "wa"), "ao"))
    out_specs = (P(("ia", "wa"), "ao"), P(("ia", "ao"), "wa"), P("wa", "ia", "ao"))
    return jax.shard_map(
        per_device, mesh=mesh, in_specs=in_specs, out_specs=out_specs, check_vma=False
    )
```

time: 379 us -> 125 us (0.33)
  waiting for transfers between devices: 333 us -> 0 us
  Pallas kernels: 0 us -> 115 us
  matrix products: 28.2 us -> 0 us
  between operations: 13.8 us -> 0.66 us
  local copies, waits for them, and re-layouts: 0.02 us -> 7.3 us
    all_gather x2 -> x0, waiting for transfers between devices: 141 us -> none  [the longest x1 78.8 us: per_device(): weight = lax.all_gather(proj_weight, 'ia', axis=1, tiled=True)[0]]
    pallas_call x0 -> x1, Pallas kernels: none -> 115 us  [per_device(): pl.pallas_call(kernel, out_shape=(shape((TOK, D_ROW), BF16), shape((8, 64...]
    reduce_scatter x2 -> x0, waiting for transfers between devices: 106 us -> none  [the longest x1 75.5 us: per_device(): lax.psum_scatter(jnp.dot(subset, weight, preferred_element_type=jnp.float...]
    unnamed x6 -> x0, waiting for transfers between devices: 86.3 us -> none
    dot_general x3 -> x0, matrix products: 28.2 us -> none  [the longest x1 10.8 us: per_device(): lax.dot_general(subset, weight, (((1,), (1,)), ((), ())), preferred_eleme...]
    unnamed x6 -> x5, local copies, waits for them, and re-layouts: 0.02 us -> 5.08 us
  transfers between devices with their start and end apart: 5 -> 0, of which waited for: 5 -> 0; matrix products, arithmetic and copies ran while one was open for 8% -> 0% of each run, Pallas kernels for 0% -> 0%
where the time goes in v1:
time: 125 us; the launch traced here: 123 us
  Pallas kernels  115 us (92%)
  local copies, waits for them, and re-layouts  7.3 us (6%)
    pallas_call x1, Pallas kernels, per_device(): pl.pallas_call(kernel, out_shape=(shape((TOK, D_ROW), BF16), shape((8, 64...  115 us
    unnamed x5, local copies, waits for them, and re-layouts  5.08 us

profile of v1, /device:TPU:65, one launch (start us, length us, event | category | flops | bytes accessed | tf_op | source)
XLA Modules:
  0.0 122.9 jit_solution(7039869747682676283)
XLA Ops:
  0.6 2.2 %copy.8.ctx_ref = bf16[256,1856]{1,0:T(8,128)(2,1)} copy(bf16[256,1856]{0,1:T(8,128)(2,1)} %param.5) | data formatting | bytes 1900544 | tf_op args[1]
  2.9 114.9 %shard_map.67 = (bf16[32,3712]{1,0:T(8,128)(2,1)}, bf16[8,64,256]{2,1,0:T(8,128)(2,1)}, bf16[232,3712]{1,0:T(8,128)(2,1)}) custom-call(bf16[32,3712]{1,0:T(8,128)(2,1)} %res_ref.1, bf16[256,1856]{1,0:T(8,128)(2,1)} %copy.8.ctx_ref, bf16[232,3712]{1,0:T(8,128)(2,1)} %bitcast.5, bf16[32,3712]{1,0:T(8,128)(2,1)} %g_ref.1), custom_call_target="tpu_custom_call" | custom-call | flops 10947133440 | bytes 8388608 | tf_op jit(solution)/shard_map/pallas_call | solution.py:434
  117.8 0.0 copy-start
  117.8 1.1 slice_bitcast_fusion
  118.9 0.2 copy.9
  119.0 1.0 reshape.9
  120.0 1.6 %copy.12 = bf16[32,3712]{1,0:T(8,128)(2,1)} copy(bf16[32,3712]{1,0:T(8,128)(2,1)} %get-tuple-element.12) | data formatting | bytes 475136
  121.7 0.0 copy-done
  121.7 1.2 copy.13
Async XLA Ops:
  117.8 3.9 %copy-start = (bf16[232,3712]{1,0:T(8,128)(2,1)S(1)}, bf16[232,3712]{1,0:T(8,128)(2,1)}, u32[]{:S(2)}) copy-start(bf16[232,3712]{1,0:T(8,128)(2,1)} %get-tuple-element.8) | copy-start | bytes 5167108

commit v2 on v1

v2 whole, which is shorter than its diff:
```python
import jax
import jax.numpy as jnp
from jax import lax
from jax.experimental import pallas as pl
from jax.experimental.pallas import tpu as pltpu
from jax.sharding import PartitionSpec as P

MESH = pl.DeviceIdType.MESH
BF16 = jnp.bfloat16
F32 = jnp.float32

ROWS = 232
D_ROW = 3712
SHIFT = 1792
WIN = 1920
NC = 3
CW = WIN // NC
TOK = 32


class Sems:
    def __init__(self):
        self.n = 0

    def take(self, count):
        base = self.n
        self.n += count
        return base


N_SEMS = 224


def kernel(
    res_ref, ctx_ref, w_ref, g_ref,
    upd_ref, cg_ref, wg_ref,
    Wb, Gb, Xb, XT,
    bufA, RA, bufB1, bufB2, RB1, RB2, PF, accP,
    bufY, RY, bufZ, RZ, bufC, RC, own,
    OWN, DY, RDY, RDC, TZ, RDZ,
    DWs, RW,
    ss, rs, ls,
):
    ia = lax.axis_index("ia")
    wa = lax.axis_index("wa")
    zl = lax.axis_index("ao")
    y, c = lax.div(ia, 2), lax.rem(ia, 2)
    x, zh = lax.div(wa, 2), lax.rem(wa, 2)
    oc, zn = 1 - c, 1 - zh

    def flip(v):
        return v + 1 - 2 * lax.rem(v, 2)

    ya, yb = flip(y), 3 - y

    def w_pair(yy, cc):
        return (1 - cc) * flip(yy) + cc * (3 - yy)

    def t_pair(yy, cc):
        return cc * flip(yy) + (1 - cc) * (3 - yy)

    wp, tp = w_pair(y, c), t_pair(y, c)
    xp, xm, x2 = lax.rem(x + 1, 4), lax.rem(x + 3, 4), lax.rem(x + 2, 4)

    def dev(yy=y, cc=c, xx=x, hh=zh, ll=zl):
        return (2 * yy + cc, 2 * xx + hh, ll)

    other_core = dev(cc=oc)
    partners = [
        other_core,
        dev(yy=ya, cc=0), dev(yy=ya, cc=1), dev(yy=yb, cc=0), dev(yy=yb, cc=1),
        dev(xx=xp), dev(xx=xm),
        dev(hh=zn), dev(hh=zn, cc=oc),
    ] + [dev(ll=lax.rem(zl + m, 4)) for m in (1, 2, 3)]

    barrier = pltpu.get_barrier_semaphore()
    for p in partners:
        pl.semaphore_signal(barrier, inc=1, device_id=p, device_id_type=MESH)
    pl.semaphore_wait(barrier, len(partners))

    s_idx, r_idx, l_idx = Sems(), Sems(), Sems()
    sent = []

    def send(src, dst, r, to, s=None):
        if s is None:
            s = s_idx.take(1)
        cp = pltpu.make_async_remote_copy(
            src_ref=src, dst_ref=dst, send_sem=ss.at[s], recv_sem=rs.at[r],
            device_id=to, device_id_type=MESH,
        )
        cp.start()
        return cp

    def post(*args):
        sent.append(send(*args))

    def got(dst, r):
        pltpu.make_async_remote_copy(
            src_ref=dst, dst_ref=dst, send_sem=ss.at[0], recv_sem=rs.at[r],
            device_id=other_core, device_id_type=MESH,
        ).wait_recv()

    def local(src, dst):
        cp = pltpu.make_async_copy(src, dst, ls.at[l_idx.take(1)])
        cp.start()
        return cp

    def window(cc):
        return pl.ds(pl.multiple_of(cc * SHIFT, 128), WIN)

    r_g0 = r_idx.take(2)
    r_g1 = r_idx.take(2)
    g_own = g_ref.at[:, window(c)]
    g_oth = g_ref.at[:, window(oc)]
    g_local = local(g_own, Gb.at[0, c, x, zh])
    post(g_oth, Gb.at[0, c, x, zh], r_g0 + c, other_core)
    post(g_own, Gb.at[0, c, x, zh], r_g1 + c, dev(hh=zn))
    post(g_oth, Gb.at[0, c, x, zh], r_g1 + c, dev(hh=zn, cc=oc))

    r_w = r_idx.take(4 * NC)

    def w_cols(cc, j):
        return pl.ds(pl.multiple_of(cc * SHIFT + j * CW, 128), CW)

    w_locals = []
    for j in range(NC):
        cols = pl.ds(j * CW, CW)
        w_locals.append(local(w_ref.at[:, w_cols(c, j)], Wb.at[c, :, cols]))
        post(w_ref.at[:, w_cols(oc, j)], Wb.at[c, :, cols], r_w + c * NC + j, other_core)

    def send_w(j):
        cols = pl.ds(j * CW, CW)
        for cc, yy in ((0, ya), (1, yb)):
            post(w_ref.at[:, w_cols(cc, j)], Wb.at[2 + c, :, cols],
                 r_w + (2 + c) * NC + j, dev(yy=yy, cc=cc))

    r_y = r_idx.take(4)
    r_xp = r_idx.take(4)
    r_xm = r_idx.take(4)
    r_f = r_idx.take(4)

    def unit(p, xx, h):
        return Gb.at[p, :, xx, h]

    def to_x(p, k, h):
        post(unit(p, x, h), unit(p, x, h), r_xp + 2 * p + k, dev(xx=xp))
        post(unit(p, x, h), unit(p, x, h), r_xm + 2 * p + k, dev(xx=xm))

    def forward_up(k, h):
        got(unit(0, xm, h), r_xp + k)
        post(unit(0, xm, h), unit(0, xm, h), r_f + k, dev(xx=xp))

    def forward_down(k, h):
        got(unit(1, xp, h), r_xm + 2 + k)
        post(unit(1, xp, h), unit(1, xp, h), r_f + 2 + k, dev(xx=xm))

    def to_partner(k, h):
        for core in range(2):
            post(Gb.at[0, core, x, h], Gb.at[1, core, x, h], r_y + 2 * k + core, dev(yy=tp))

    def from_partner(k, h):
        for core in range(2):
            got(Gb.at[1, core, x, h], r_y + 2 * k + core)

    g_local.wait()
    got(Gb.at[0, oc, x, zh], r_g0 + oc)
    to_partner(0, zh)
    to_x(0, 0, zh)

    r_c = r_idx.take(8)
    half = lax.rem(zl, 2)

    def x_block(q, blk):
        return XT.at[pl.ds(2 * q, 2), :, pl.ds(pl.multiple_of(blk * 256, 256), 256)]

    def x_group(q, yy, cc):
        chip = (1 - q) * yy + q * w_pair(yy, cc)
        return ctx_ref.at[pl.ds(2 * chip, 2)]

    def got_x(q, blk):
        got(x_block(q, blk), r_c + 2 * blk + q)

    def transpose_x(s, blk):
        t = XT[s, :, blk * 256:(blk + 1) * 256].T
        Xb[s, blk] = t.reshape(4, 64, ROWS)

    for y_to, cc in ((yb, 0), (ya, 1)):
        post(x_group(half, y_to, cc), x_block(half, 2 + c), r_c + 2 * (2 + c) + half, dev(yy=y_to, cc=cc))
    x_locals = []
    for q in range(2):
        x_locals.append(local(x_group(q, y, c), x_block(q, c)))
        post(x_group(q, y, oc), x_block(q, c), r_c + 2 * c + q, other_core)

    from_partner(0, zh)
    to_x(1, 0, zh)
    send_w(0)
    for cp in x_locals:
        cp.wait()
    for q in range(2):
        got_x(q, oc)
    for blk in range(2):
        for sl in range(4):
            transpose_x(sl, blk)
    for blk in (2, 3):
        got_x(half, blk)
        post(x_block(half, blk), x_block(half, blk), r_c + 2 * blk + half, dev(ll=flip(zl)))
    for blk in (2, 3):
        for sl in range(2):
            transpose_x(2 * half + sl, blk)
    forward_up(0, zh)
    forward_down(0, zh)

    for core in range(2):
        got(Gb.at[0, core, x, zn], r_g1 + core)
    to_partner(1, zn)
    to_x(0, 1, zn)
    send_w(1)
    from_partner(1, zn)
    to_x(1, 1, zn)
    send_w(2)

    for blk in (2, 3):
        got_x(1 - half, blk)
        for sl in range(2):
            transpose_x(2 * (1 - half) + sl, blk)
    for cp in w_locals:
        cp.wait()

    def project(j):
        total = None
        for sl in range(4):
            a = Xb[sl].reshape(1024, ROWS)
            part = jnp.dot(a, Wb[sl, :, j * CW:(j + 1) * CW], preferred_element_type=F32)
            total = part if total is None else total + part
        PF[j] = total.reshape(2, 2, 4, 64, CW)

    r_a = r_idx.take(2 * NC)
    r_b1 = r_idx.take(2 * NC)
    r_b2 = r_idx.take(2 * NC)
    to_xp, to_xm = dev(xx=xp), dev(xx=xm)

    def drain(src, s):
        pltpu.make_async_remote_copy(
            src_ref=src, dst_ref=src, send_sem=ss.at[s], recv_sem=rs.at[0],
            device_id=other_core, device_id_type=MESH,
        ).wait_send()

    def got_w(j):
        cols = pl.ds(j * CW, CW)
        got(Wb.at[oc, :, cols], r_w + oc * NC + j)
        for s in (2, 3):
            got(Wb.at[s, :, cols], r_w + s * NC + j)
        if j == 0:
            keep = (c == 0).astype(BF16)
            for s in range(4):
                Wb[s, :, 0:128] = Wb[s, :, 0:128] * keep

    def project_chunk(j):
        got_w(j)
        project(j)

    def post_a(j):
        bufA[j] = PF[j, :, :, x2].astype(BF16)
        post(bufA.at[j, 0], RA.at[j, 0], r_a + 2 * j, to_xp)
        post(bufA.at[j, 1], RA.at[j, 1], r_a + 2 * j + 1, to_xm)

    def post_b(j):
        bufB1[j, 1] = PF[j, 1, :, xp].astype(BF16)
        post(bufB1.at[j, 1], RB1.at[j, 1], r_b1 + 2 * j + 1, to_xp)
        bufB2[j, 0] = PF[j, 0, :, xm].astype(BF16)
        post(bufB2.at[j, 0], RB2.at[j, 0], r_b2 + 2 * j, to_xm)

    def pass_on(j):
        got(RA.at[j, 0], r_a + 2 * j)
        bufB1[j, 0] = (PF[j, 0, :, xp] + RA[j, 0].astype(F32)).astype(BF16)
        post(bufB1.at[j, 0], RB1.at[j, 0], r_b1 + 2 * j, to_xp)
        got(RA.at[j, 1], r_a + 2 * j + 1)
        bufB2[j, 1] = (PF[j, 1, :, xm] + RA[j, 1].astype(F32)).astype(BF16)
        post(bufB2.at[j, 1], RB2.at[j, 1], r_b2 + 2 * j + 1, to_xm)

    r_dy, r_dc, r_dz = r_idx.take(4), r_idx.take(16), r_idx.take(4)
    s_dz = s_idx.take(4)
    blocks = (x, xp, xm, x2)

    def back(k):
        d = blocks[k]

        @pl.loop(0, 4)
        def _(s):
            g = Gb[:, :, d].reshape(256, WIN)
            t = lax.dot_general(g, Wb[s], (((1,), (1,)), ((), ())),
                                preferred_element_type=F32).astype(BF16)
            t = jnp.concatenate([t, jnp.zeros((256, 256 - ROWS), BF16)], axis=1)
            t = t.reshape(2, 2, 64, 256)
            OWN[k, s] = t[0]
            DY[k, s] = t[1]

        post(DY.at[k], RDY.at[k], r_dy + k, dev(yy=tp))

    r_wg = r_idx.take(4 * NC)
    s_wg = s_idx.take(3 * NC)

    def grad(s, j):
        cols = pl.ds(pl.multiple_of(j * CW, 128), CW)
        b = Gb[:, :, :, :, :, cols].reshape(1024, CW)
        return jnp.dot(XT[s], b, preferred_element_type=F32).astype(BF16)

    own_groups = (y, wp)
    got_groups = (tp, w_pair(tp, c))

    def to_core(k):
        got(RDY.at[k], r_dy + k)
        for q in range(2):
            for part, group in ((OWN, own_groups[q]), (RDY, got_groups[q])):
                post(part.at[k, pl.ds(2 * q, 2), oc], RDC.at[k, group],
                     r_dc + 4 * k + group, other_core)

    def to_ao(k):
        d = blocks[k]
        for group in range(4):
            got(RDC.at[k, group], r_dc + 4 * k + group)
        for q in range(2):
            for part, group in ((OWN, own_groups[q]), (RDY, got_groups[q])):
                TZ[k, group] = (part[k, 2 * q:2 * q + 2, c].astype(F32)
                                + RDC[k, group].astype(F32)).astype(BF16)

        @pl.when(d != zl)
        def _():
            send(TZ.at[k], RDZ.at[zl], r_dz + zl, dev(ll=d), s_dz + k)

        @pl.when(d == zl)
        def _():
            RDZ[zl] = TZ[k]

    def grad_other(core):
        to = dev(yy=wp, cc=core)

        @pl.loop(0, NC)
        def _(j):
            DWs[core, j] = grad(2 + core, j)
            send(DWs.at[core, j], RW.at[c, 1, j], r_wg + (2 * c + 1) * NC + j, to, s_wg + core * NC + j)

    def grad_own():
        @pl.loop(0, NC)
        def _(j):
            DWs[2, j] = grad(oc, j)
            send(DWs.at[2, j], RW.at[c, 0, j], r_wg + 2 * c * NC + j, other_core, s_wg + 2 * NC + j)

        @pl.loop(0, NC)
        def _(j):
            RW[c, 0, j] = grad(c, j)

    project_chunk(0)
    forward_up(1, zn)
    forward_down(1, zn)
    post_a(0)
    got_w(1)
    got_w(2)
    back(0)
    project(1)
    for h, k in ((zh, 0), (zn, 1)):
        got(unit(1, xm, h), r_xp + 2 + k)
        got(unit(0, xp, h), r_xm + k)
    back(1)
    to_core(0)
    post_b(0)
    back(2)
    post_a(1)
    for k, h in ((0, zh), (1, zn)):
        got(unit(0, x2, h), r_f + k)
        got(unit(1, x2, h), r_f + 2 + k)
    back(3)
    to_ao(0)
    post_b(1)
    grad_other(0)
    to_core(1)
    grad_other(1)
    pass_on(0)
    to_ao(1)
    to_core(2)
    project(2)
    post_a(2)
    post_b(2)
    to_ao(2)
    to_core(3)
    pass_on(1)
    to_ao(3)
    grad_own()
    pass_on(2)

    r_py, r_pz, r_pc = r_idx.take(8 * NC), r_idx.take(4 * NC), r_idx.take(NC)

    def to_y(j):
        got(RB1.at[j, 1], r_b1 + 2 * j + 1)
        got(RB2.at[j, 1], r_b2 + 2 * j + 1)
        v = PF[j, 1, :, x] + RB1[j, 1].astype(F32) + RB2[j, 1].astype(F32)
        bufY[j] = v.astype(BF16).reshape(8, 16, CW)
        for h in range(8):
            post(bufY.at[j, h], RY.at[j, h], r_py + 8 * j + h, dev(yy=tp))

    def to_z(j):
        got(RB1.at[j, 0], r_b1 + 2 * j)
        got(RB2.at[j, 0], r_b2 + 2 * j)
        v = PF[j, 0, :, x] + RB1[j, 0].astype(F32) + RB2[j, 0].astype(F32)
        for h in range(8):
            got(RY.at[j, h], r_py + 8 * j + h)
        v = v.reshape(2, 2, TOK, CW) + RY[j].astype(F32).reshape(2, 2, TOK, CW)
        accP[j] = v
        bufZ[j] = accP[j, :, zn].astype(BF16).reshape(4, 16, CW)
        for h in range(4):
            post(bufZ.at[j, h], RZ.at[j, h], r_pz + 4 * j + h, dev(hh=zn))

    def to_c(j):
        for h in range(4):
            got(RZ.at[j, h], r_pz + 4 * j + h)
        own[j] = accP[j, c, zh] + RZ[j, pl.ds(2 * c, 2)].astype(F32).reshape(TOK, CW)
        bufC[j] = accP[j, oc, zh] + RZ[j, pl.ds(2 * oc, 2)].astype(F32).reshape(TOK, CW)
        post(bufC.at[j], RC.at[j], r_pc + j, other_core)

    def finish_context_grad():
        for m in (1, 2, 3):
            src = lax.rem(zl + m, 4)
            got(RDZ.at[src], r_dz + src)
        total = RDZ[0].astype(F32)
        for m in (1, 2, 3):
            total = total + RDZ[m].astype(F32)
        total = total.astype(BF16).reshape(8, 64, 256)
        cg_ref[...] = jnp.concatenate([total[g][:, :ROWS] for g in range(8)], axis=1)

    to_y(0)
    to_y(1)
    to_z(0)
    to_y(2)
    to_z(1)
    to_c(0)
    to_z(2)
    to_c(1)
    finish_context_grad()
    to_c(2)

    @pl.loop(0, NC)
    def _(j):
        got(RW.at[oc, 0, j], r_wg + 2 * oc * NC + j)
        for w in range(2):
            got(RW.at[w, 1, j], r_wg + (2 * w + 1) * NC + j)

    for w in range(2):
        @pl.loop(0, NC)
        def _(j):
            cols = pl.ds(pl.multiple_of(w * SHIFT + j * CW, 128), CW)
            wg_ref[:, cols] = (RW[w, 0, j].astype(F32) + RW[w, 1, j].astype(F32)).astype(BF16)

    for j in range(NC):
        got(RC.at[j], r_pc + j)
    for w in (1, 0):
        for j in range(NC):
            cols = slice(w * SHIFT + j * CW, w * SHIFT + (j + 1) * CW)
            v = jnp.where(c == w, own[j], RC[j])
            upd_ref[:, cols] = (res_ref[:, cols].astype(F32) + v).astype(BF16)

    for cp in sent:
        cp.wait_send()
    for j in range(NC):
        for s in range(3):
            drain(DWs.at[s, j], s_wg + s * NC + j)
    for k in range(4):
        @pl.when(blocks[k] != zl)
        def _():
            drain(TZ.at[k], s_dz + k)


def hand_over(a, b, d, a_out, b_out, d_out):
    a_out[...] = a[...]
    b_out[...] = b[...]
    d_out[...] = d[...]


def per_device(residual, context, proj_weight, out_grad):
    vmem = pl.BlockSpec(memory_space=pltpu.VMEM)
    anywhere = pl.BlockSpec(memory_space=pl.ANY)
    shape = jax.ShapeDtypeStruct
    updated, context_grad, weight_grad = pl.pallas_call(
        kernel,
        out_shape=(
            shape((TOK, D_ROW), BF16),
            shape((64, 8 * ROWS), BF16),
            shape((ROWS, D_ROW), BF16),
        ),
        in_specs=[vmem, anywhere, anywhere, anywhere],
        out_specs=(vmem, vmem, vmem),
        scratch_shapes=[
            pltpu.VMEM((4, ROWS, WIN), BF16),
            pltpu.VMEM((2, 2, 4, 2, TOK, WIN), BF16),
            pltpu.VMEM((4, 4, 4, 64, ROWS), BF16),
            pltpu.VMEM((4, ROWS, 1024), BF16),
            pltpu.VMEM((NC, 2, 2, 64, CW), BF16),
            pltpu.VMEM((NC, 2, 2, 64, CW), BF16),
            pltpu.VMEM((NC, 2, 2, 64, CW), BF16),
            pltpu.VMEM((NC, 2, 2, 64, CW), BF16),
            pltpu.VMEM((NC, 2, 2, 64, CW), BF16),
            pltpu.VMEM((NC, 2, 2, 64, CW), BF16),
            pltpu.VMEM((NC, 2, 2, 4, 64, CW), F32),
            pltpu.VMEM((NC, 2, 2, TOK, CW), F32),
            pltpu.VMEM((NC, 8, 16, CW), BF16),
            pltpu.VMEM((NC, 8, 16, CW), BF16),
            pltpu.VMEM((NC, 4, 16, CW), BF16),
            pltpu.VMEM((NC, 4, 16, CW), BF16),
            pltpu.VMEM((NC, TOK, CW), F32),
            pltpu.VMEM((NC, TOK, CW), F32),
            pltpu.VMEM((NC, TOK, CW), F32),
            pltpu.VMEM((4, 4, 2, 64, 256), BF16),
            pltpu.VMEM((4, 4, 2, 64, 256), BF16),
            pltpu.VMEM((4, 4, 2, 64, 256), BF16),
            pltpu.VMEM((4, 4, 2, 64, 256), BF16),
            pltpu.VMEM((4, 4, 2, 64, 256), BF16),
            pltpu.VMEM((4, 4, 2, 64, 256), BF16),
            pltpu.VMEM((3, NC, ROWS, CW), BF16),
            pltpu.VMEM((2, 2, NC, ROWS, CW), BF16),
            pltpu.SemaphoreType.DMA((N_SEMS,)),
            pltpu.SemaphoreType.DMA((N_SEMS,)),
            pltpu.SemaphoreType.DMA((16,)),
        ],
        compiler_params=pltpu.CompilerParams(
            collective_id=0, has_side_effects=True, vmem_limit_bytes=60 * 2**20
        ),
        cost_estimate=pl.CostEstimate(
            flops=6 * 1024 * 928 * WIN, bytes_accessed=8 * 2**20, transcendentals=0
        ),
    )(residual, context.T.reshape(8, ROWS, 256), proj_weight[0], out_grad)
    updated, context_grad, weight_grad = pl.pallas_call(
        hand_over,
        out_shape=(
            shape((TOK, D_ROW), BF16),
            shape((64, 8 * ROWS), BF16),
            shape((ROWS, D_ROW), BF16),
        ),
        in_specs=[vmem] * 3,
        out_specs=(vmem,) * 3,
    )(updated, context_grad, weight_grad)
    return updated, context_grad, weight_grad[None]


def solution(mesh):
    in_specs = (P(("ia", "wa"), "ao"), P("ia", "wa"), P("wa", "ia", "ao"), P(("ia", "wa"), "ao"))
    out_specs = (P(("ia", "wa"), "ao"), P(("ia", "ao"), "wa"), P("wa", "ia", "ao"))
    return jax.shard_map(
        per_device, mesh=mesh, in_specs=in_specs, out_specs=out_specs, check_vma=False
    )
```

time: 125 us -> 109 us (0.87)
  the two profiles are of different devices: /device:TPU:65 before, /device:TPU:45 now
where the time goes in v2:
time: 109 us; the launch traced here: 108 us
  Pallas kernels  108 us (99%)
    pallas_call x1, Pallas kernels, per_device(): pl.pallas_call(kernel, out_shape=(shape((TOK, D_ROW), BF16), shape((64, 8...  105 us
    pallas_call x1, Pallas kernels, per_device(): pl.pallas_call(hand_over, out_shape=(shape((TOK, D_ROW), BF16), shape((64...  3.09 us

profile of v2, /device:TPU:45, one launch (start us, length us, event | category | flops | bytes accessed | tf_op | source)
XLA Modules:
  0.0 108.4 jit_solution(2391464066492447644)
XLA Ops:
  0.6 104.6 %shard_map.67 = (bf16[32,3712]{1,0:T(8,128)(2,1)}, bf16[64,1856]{1,0:T(8,128)(2,1)}, bf16[232,3712]{1,0:T(8,128)(2,1)}) custom-call(bf16[32,3712]{1,0:T(8,128)(2,1)} %res_ref.1, bf16[8,232,256]{2,1,0:T(8,128)(2,1)} %bitcast.7, bf16[232,3712]{1,0:T(8,128)(2,1)} %bitcast.5, bf16[32,3712]{1,0:T(8,128)(2,1)} %g_ref.1), custom_call_target="tpu_custom_call" | custom-call | flops 10947133440 | bytes 8388608 | tf_op jit(solution)/shard_map/pallas_call | solution.py:482
  105.3 3.1 %shard_map.68 = (bf16[32,3712]{1,0:T(8,128)(2,1)}, bf16[64,1856]{1,0:T(8,128)(2,1)}, bf16[232,3712]{1,0:T(8,128)(2,1)}) custom-call(bf16[32,3712]{1,0:T(8,128)(2,1)} %get-tuple-element.9.a, bf16[64,1856]{1,0:T(8,128)(2,1)} %get-tuple-element.10.b, bf16[232,3712]{1,0:T(8,128)(2,1)} %get-tuple-element.11.d), custom_call_target="tpu_custom_call" | custom-call | tf_op jit(solution)/shard_map/pallas_call | solution.py:530

commit v3 on v2

--- a/solution.py
+++ b/solution.py
@@ -15,6 +15,8 @@
 WIN = 1920
 NC = 3
 CW = WIN // NC
+PW = (768, 768, 384)
+PO = (0, 768, 1536)
 TOK = 32
 
 
@@ -37,8 +39,8 @@
     Wb, Gb, Xb, XT,
     bufA, RA, bufB1, bufB2, RB1, RB2, PF, accP,
     bufY, RY, bufZ, RZ, bufC, RC, own,
-    OWN, DY, RDY, RDC, TZ, RDZ,
-    DWs, RW,
+    OWN, DY, RDY, RDC, TZ, RDZ, RL,
+    DWs, RW, WG,
     ss, rs, ls,
 ):
     ia = lax.axis_index("ia")
@@ -72,6 +74,13 @@
         dev(xx=xp), dev(xx=xm),
         dev(hh=zn), dev(hh=zn, cc=oc),
     ] + [dev(ll=lax.rem(zl + m, 4)) for m in (1, 2, 3)]
+
+    middle = lax.rem(zl, 3) != 0
+    far = 3 * (1 - lax.rem(zl + 1, 2))
+
+    @pl.when(jnp.logical_not(middle))
+    def _():
+        RDZ[3 - zl] = jnp.zeros((4, 2, 64, 256), BF16)
 
     barrier = pltpu.get_barrier_semaphore()
     for p in partners:
@@ -120,21 +129,15 @@
     r_w = r_idx.take(4 * NC)
 
     def w_cols(cc, j):
-        return pl.ds(pl.multiple_of(cc * SHIFT + j * CW, 128), CW)
-
-    w_locals = []
-    for j in range(NC):
-        cols = pl.ds(j * CW, CW)
-        w_locals.append(local(w_ref.at[:, w_cols(c, j)], Wb.at[c, :, cols]))
-        post(w_ref.at[:, w_cols(oc, j)], Wb.at[c, :, cols], r_w + c * NC + j, other_core)
+        return pl.ds(pl.multiple_of(cc * SHIFT + PO[j], 128), PW[j])
 
     def send_w(j):
-        cols = pl.ds(j * CW, CW)
+        cols = pl.ds(PO[j], PW[j])
         for cc, yy in ((0, ya), (1, yb)):
             post(w_ref.at[:, w_cols(cc, j)], Wb.at[2 + c, :, cols],
                  r_w + (2 + c) * NC + j, dev(yy=yy, cc=cc))
 
-    r_y = r_idx.take(4)
+    r_y = r_idx.take(2)
     r_xp = r_idx.take(4)
     r_xm = r_idx.take(4)
     r_f = r_idx.take(4)
@@ -155,12 +158,10 @@
         post(unit(1, xp, h), unit(1, xp, h), r_f + 2 + k, dev(xx=xm))
 
     def to_partner(k, h):
-        for core in range(2):
-            post(Gb.at[0, core, x, h], Gb.at[1, core, x, h], r_y + 2 * k + core, dev(yy=tp))
+        post(unit(0, x, h), unit(1, x, h), r_y + k, dev(yy=tp))
 
     def from_partner(k, h):
-        for core in range(2):
-            got(Gb.at[1, core, x, h], r_y + 2 * k + core)
+        got(unit(1, x, h), r_y + k)
 
     g_local.wait()
     got(Gb.at[0, oc, x, zh], r_g0 + oc)
@@ -191,9 +192,17 @@
         x_locals.append(local(x_group(q, y, c), x_block(q, c)))
         post(x_group(q, y, oc), x_block(q, c), r_c + 2 * c + q, other_core)
 
+    w_locals = []
+    for j in range(NC):
+        cols = pl.ds(PO[j], PW[j])
+        w_locals.append(local(w_ref.at[:, w_cols(c, j)], Wb.at[c, :, cols]))
+        post(w_ref.at[:, w_cols(oc, j)], Wb.at[c, :, cols], r_w + c * NC + j, other_core)
+
+
     from_partner(0, zh)
     to_x(1, 0, zh)
     send_w(0)
+    forward_up(0, zh)
     for cp in x_locals:
         cp.wait()
     for q in range(2):
@@ -207,7 +216,6 @@
     for blk in (2, 3):
         for sl in range(2):
             transpose_x(2 * half + sl, blk)
-    forward_up(0, zh)
     forward_down(0, zh)
 
     for core in range(2):
@@ -215,9 +223,9 @@
     to_partner(1, zn)
     to_x(0, 1, zn)
     send_w(1)
+    send_w(2)
     from_partner(1, zn)
     to_x(1, 1, zn)
-    send_w(2)
 
     for blk in (2, 3):
         got_x(1 - half, blk)
@@ -225,14 +233,18 @@
             transpose_x(2 * (1 - half) + sl, blk)
     for cp in w_locals:
         cp.wait()
+    for j in range(NC):
+        got(Wb.at[oc, :, pl.ds(PO[j], PW[j])], r_w + oc * NC + j)
 
     def project(j):
-        total = None
-        for sl in range(4):
-            a = Xb[sl].reshape(1024, ROWS)
-            part = jnp.dot(a, Wb[sl, :, j * CW:(j + 1) * CW], preferred_element_type=F32)
-            total = part if total is None else total + part
-        PF[j] = total.reshape(2, 2, 4, 64, CW)
+        @pl.loop(0, 4)
+        def _(blk):
+            total = None
+            for sl in range(4):
+                a = Xb[sl, blk].reshape(256, ROWS)
+                part = jnp.dot(a, Wb[sl, :, PO[j]:PO[j] + PW[j]], preferred_element_type=F32)
+                total = part if total is None else total + part
+            PF[j][blk] = total.reshape(4, 64, PW[j])
 
     r_a = r_idx.take(2 * NC)
     r_b1 = r_idx.take(2 * NC)
@@ -246,8 +258,7 @@
         ).wait_send()
 
     def got_w(j):
-        cols = pl.ds(j * CW, CW)
-        got(Wb.at[oc, :, cols], r_w + oc * NC + j)
+        cols = pl.ds(PO[j], PW[j])
         for s in (2, 3):
             got(Wb.at[s, :, cols], r_w + s * NC + j)
         if j == 0:
@@ -260,32 +271,33 @@
         project(j)
 
     def post_a(j):
-        bufA[j] = PF[j, :, :, x2].astype(BF16)
-        post(bufA.at[j, 0], RA.at[j, 0], r_a + 2 * j, to_xp)
-        post(bufA.at[j, 1], RA.at[j, 1], r_a + 2 * j + 1, to_xm)
+        bufA[j][...] = PF[j][:, x2].astype(BF16).reshape(2, 2, 64, PW[j])
+        post(bufA[j].at[0], RA[j].at[0], r_a + 2 * j, to_xp)
+        post(bufA[j].at[1], RA[j].at[1], r_a + 2 * j + 1, to_xm)
 
     def post_b(j):
-        bufB1[j, 1] = PF[j, 1, :, xp].astype(BF16)
-        post(bufB1.at[j, 1], RB1.at[j, 1], r_b1 + 2 * j + 1, to_xp)
-        bufB2[j, 0] = PF[j, 0, :, xm].astype(BF16)
-        post(bufB2.at[j, 0], RB2.at[j, 0], r_b2 + 2 * j, to_xm)
+        bufB1[j][1] = PF[j][2:4, xp].astype(BF16)
+        post(bufB1[j].at[1], RB1[j].at[1], r_b1 + 2 * j + 1, to_xp)
+        bufB2[j][0] = PF[j][0:2, xm].astype(BF16)
+        post(bufB2[j].at[0], RB2[j].at[0], r_b2 + 2 * j, to_xm)
 
     def pass_on(j):
-        got(RA.at[j, 0], r_a + 2 * j)
-        bufB1[j, 0] = (PF[j, 0, :, xp] + RA[j, 0].astype(F32)).astype(BF16)
-        post(bufB1.at[j, 0], RB1.at[j, 0], r_b1 + 2 * j, to_xp)
-        got(RA.at[j, 1], r_a + 2 * j + 1)
-        bufB2[j, 1] = (PF[j, 1, :, xm] + RA[j, 1].astype(F32)).astype(BF16)
-        post(bufB2.at[j, 1], RB2.at[j, 1], r_b2 + 2 * j + 1, to_xm)
+        got(RA[j].at[0], r_a + 2 * j)
+        bufB1[j][0] = (PF[j][0:2, xp] + RA[j][0].astype(F32)).astype(BF16)
+        post(bufB1[j].at[0], RB1[j].at[0], r_b1 + 2 * j, to_xp)
+        got(RA[j].at[1], r_a + 2 * j + 1)
+        bufB2[j][1] = (PF[j][2:4, xm] + RA[j][1].astype(F32)).astype(BF16)
+        post(bufB2[j].at[1], RB2[j].at[1], r_b2 + 2 * j + 1, to_xm)
 
     r_dy, r_dc, r_dz = r_idx.take(4), r_idx.take(16), r_idx.take(4)
-    s_dz = s_idx.take(4)
+    r_rl = r_idx.take(1)
+    s_dz = s_idx.take(5)
     blocks = (x, xp, xm, x2)
 
-    def back(k):
+    def back(k, first=0, last=4):
         d = blocks[k]
 
-        @pl.loop(0, 4)
+        @pl.loop(first, last)
         def _(s):
             g = Gb[:, :, d].reshape(256, WIN)
             t = lax.dot_general(g, Wb[s], (((1,), (1,)), ((), ())),
@@ -295,7 +307,8 @@
             OWN[k, s] = t[0]
             DY[k, s] = t[1]
 
-        post(DY.at[k], RDY.at[k], r_dy + k, dev(yy=tp))
+        if last == 4:
+            post(DY.at[k], RDY.at[k], r_dy + k, dev(yy=tp))
 
     r_wg = r_idx.take(4 * NC)
     s_wg = s_idx.take(3 * NC)
@@ -321,16 +334,30 @@
             got(RDC.at[k, group], r_dc + 4 * k + group)
         for q in range(2):
             for part, group in ((OWN, own_groups[q]), (RDY, got_groups[q])):
-                TZ[k, group] = (part[k, 2 * q:2 * q + 2, c].astype(F32)
+                TZ[d, group] = (part[k, 2 * q:2 * q + 2, c].astype(F32)
                                 + RDC[k, group].astype(F32)).astype(BF16)
 
-        @pl.when(d != zl)
+        relay = jnp.logical_and(jnp.logical_not(middle), d == 3 - zl)
+        held = jnp.logical_and(middle, d == far)
+
+        @pl.when(relay)
         def _():
-            send(TZ.at[k], RDZ.at[zl], r_dz + zl, dev(ll=d), s_dz + k)
+            send(TZ.at[d], RL, r_rl, dev(ll=1 + lax.div(zl, 3)), s_dz + k)
+
+        @pl.when(jnp.logical_not(jnp.logical_or(relay, jnp.logical_or(held, d == zl))))
+        def _():
+            send(TZ.at[d], RDZ.at[zl], r_dz + zl, dev(ll=d), s_dz + k)
 
         @pl.when(d == zl)
         def _():
-            RDZ[zl] = TZ[k]
+            RDZ[zl] = TZ[d]
+
+    def relay_on():
+        @pl.when(middle)
+        def _():
+            got(RL, r_rl)
+            TZ[far] = (TZ[far].astype(F32) + RL[...].astype(F32)).astype(BF16)
+            send(TZ.at[far], RDZ.at[zl], r_dz + zl, dev(ll=far), s_dz + 4)
 
     def grad_other(core):
         to = dev(yy=wp, cc=core)
@@ -340,87 +367,101 @@
             DWs[core, j] = grad(2 + core, j)
             send(DWs.at[core, j], RW.at[c, 1, j], r_wg + (2 * c + 1) * NC + j, to, s_wg + core * NC + j)
 
-    def grad_own():
+    def grad_core():
         @pl.loop(0, NC)
         def _(j):
             DWs[2, j] = grad(oc, j)
             send(DWs.at[2, j], RW.at[c, 0, j], r_wg + 2 * c * NC + j, other_core, s_wg + 2 * NC + j)
 
+    def grad_own():
         @pl.loop(0, NC)
         def _(j):
             RW[c, 0, j] = grad(c, j)
 
     project_chunk(0)
     forward_up(1, zn)
+    post_a(0)
+    back(0, 0, 2)
     forward_down(1, zn)
-    post_a(0)
-    got_w(1)
+    post_b(0)
+    project_chunk(1)
+    post_a(1)
     got_w(2)
-    back(0)
-    project(1)
+    back(0, 2, 4)
     for h, k in ((zh, 0), (zn, 1)):
         got(unit(1, xm, h), r_xp + 2 + k)
         got(unit(0, xp, h), r_xm + k)
     back(1)
+    back(2)
+    pass_on(0)
+    post_b(1)
     to_core(0)
-    post_b(0)
-    back(2)
-    post_a(1)
     for k, h in ((0, zh), (1, zn)):
         got(unit(0, x2, h), r_f + k)
         got(unit(1, x2, h), r_f + 2 + k)
     back(3)
     to_ao(0)
-    post_b(1)
+    to_core(1)
     grad_other(0)
-    to_core(1)
-    grad_other(1)
-    pass_on(0)
     to_ao(1)
     to_core(2)
     project(2)
     post_a(2)
-    post_b(2)
+    pass_on(1)
     to_ao(2)
     to_core(3)
-    pass_on(1)
+    grad_other(1)
+    post_b(2)
     to_ao(3)
-    grad_own()
-    pass_on(2)
-
-    r_py, r_pz, r_pc = r_idx.take(8 * NC), r_idx.take(4 * NC), r_idx.take(NC)
+
+    r_py, r_pz, r_pc = r_idx.take(NC), r_idx.take(NC), r_idx.take(NC)
 
     def to_y(j):
-        got(RB1.at[j, 1], r_b1 + 2 * j + 1)
-        got(RB2.at[j, 1], r_b2 + 2 * j + 1)
-        v = PF[j, 1, :, x] + RB1[j, 1].astype(F32) + RB2[j, 1].astype(F32)
-        bufY[j] = v.astype(BF16).reshape(8, 16, CW)
-        for h in range(8):
-            post(bufY.at[j, h], RY.at[j, h], r_py + 8 * j + h, dev(yy=tp))
+        got(RB1[j].at[1], r_b1 + 2 * j + 1)
+        got(RB2[j].at[1], r_b2 + 2 * j + 1)
+        v = PF[j][2:4, x] + RB1[j][1].astype(F32) + RB2[j][1].astype(F32)
+        bufY[j][...] = v.astype(BF16).reshape(2, 2, TOK, PW[j])
+        post(bufY[j], RY[j], r_py + j, dev(yy=tp))
 
     def to_z(j):
-        got(RB1.at[j, 0], r_b1 + 2 * j)
-        got(RB2.at[j, 0], r_b2 + 2 * j)
-        v = PF[j, 0, :, x] + RB1[j, 0].astype(F32) + RB2[j, 0].astype(F32)
-        for h in range(8):
-            got(RY.at[j, h], r_py + 8 * j + h)
-        v = v.reshape(2, 2, TOK, CW) + RY[j].astype(F32).reshape(2, 2, TOK, CW)
-        accP[j] = v
-        bufZ[j] = accP[j, :, zn].astype(BF16).reshape(4, 16, CW)
-        for h in range(4):
-            post(bufZ.at[j, h], RZ.at[j, h], r_pz + 4 * j + h, dev(hh=zn))
+        got(RB1[j].at[0], r_b1 + 2 * j)
+        got(RB2[j].at[0], r_b2 + 2 * j)
+        v = PF[j][0:2, x] + RB1[j][0].astype(F32) + RB2[j][0].astype(F32)
+        got(RY[j], r_py + j)
+        v = v.reshape(2, 2, TOK, PW[j]) + RY[j][...].astype(F32)
+        accP[j][...] = v
+        bufZ[j][...] = accP[j][:, zn].astype(BF16)
+        post(bufZ[j], RZ[j], r_pz + j, dev(hh=zn))
 
     def to_c(j):
-        for h in range(4):
-            got(RZ.at[j, h], r_pz + 4 * j + h)
-        own[j] = accP[j, c, zh] + RZ[j, pl.ds(2 * c, 2)].astype(F32).reshape(TOK, CW)
-        bufC[j] = accP[j, oc, zh] + RZ[j, pl.ds(2 * oc, 2)].astype(F32).reshape(TOK, CW)
-        post(bufC.at[j], RC.at[j], r_pc + j, other_core)
+        got(RZ[j], r_pz + j)
+        own[j][...] = accP[j][c, zh] + RZ[j][c].astype(F32)
+        bufC[j][...] = accP[j][oc, zh] + RZ[j][oc].astype(F32)
+        post(bufC[j], RC[j], r_pc + j, other_core)
+
+    def finish_weight_grad():
+        @pl.loop(0, NC)
+        def _(j):
+            got(RW.at[oc, 0, j], r_wg + 2 * oc * NC + j)
+            for w in range(2):
+                got(RW.at[w, 1, j], r_wg + (2 * w + 1) * NC + j)
+
+        for w in range(2):
+            @pl.loop(0, NC)
+            def _(j):
+                cols = pl.ds(pl.multiple_of(w * SHIFT + j * CW, 128), CW)
+                WG[:, cols] = (RW[w, 0, j].astype(F32) + RW[w, 1, j].astype(F32)).astype(BF16)
+
+        return local(WG, wg_ref)
 
     def finish_context_grad():
         for m in (1, 2, 3):
             src = lax.rem(zl + m, 4)
-            got(RDZ.at[src], r_dz + src)
+
+            @pl.when(jnp.logical_or(middle, src != 3 - zl))
+            def _():
+                got(RDZ.at[src], r_dz + src)
+
         total = RDZ[0].astype(F32)
         for m in (1, 2, 3):
             total = total + RDZ[m].astype(F32)
@@ -428,45 +469,45 @@
         cg_ref[...] = jnp.concatenate([total[g][:, :ROWS] for g in range(8)], axis=1)
 
     to_y(0)
+    grad_core()
+    pass_on(2)
+    relay_on()
+    to_z(0)
     to_y(1)
-    to_z(0)
+    grad_own()
     to_y(2)
     to_z(1)
+    to_z(2)
+    wg_out = finish_weight_grad()
     to_c(0)
-    to_z(2)
     to_c(1)
     finish_context_grad()
     to_c(2)
 
-    @pl.loop(0, NC)
-    def _(j):
-        got(RW.at[oc, 0, j], r_wg + 2 * oc * NC + j)
-        for w in range(2):
-            got(RW.at[w, 1, j], r_wg + (2 * w + 1) * NC + j)
-
-    for w in range(2):
-        @pl.loop(0, NC)
-        def _(j):
-            cols = pl.ds(pl.multiple_of(w * SHIFT + j * CW, 128), CW)
-            wg_ref[:, cols] = (RW[w, 0, j].astype(F32) + RW[w, 1, j].astype(F32)).astype(BF16)
-
     for j in range(NC):
-        got(RC.at[j], r_pc + j)
+        got(RC[j], r_pc + j)
     for w in (1, 0):
         for j in range(NC):
-            cols = slice(w * SHIFT + j * CW, w * SHIFT + (j + 1) * CW)
-            v = jnp.where(c == w, own[j], RC[j])
+            cols = slice(w * SHIFT + PO[j], w * SHIFT + PO[j] + PW[j])
+            v = jnp.where(c == w, own[j][...], RC[j][...])
             upd_ref[:, cols] = (res_ref[:, cols].astype(F32) + v).astype(BF16)
 
+    wg_out.wait()
     for cp in sent:
         cp.wait_send()
     for j in range(NC):
         for s in range(3):
             drain(DWs.at[s, j], s_wg + s * NC + j)
     for k in range(4):
-        @pl.when(blocks[k] != zl)
+        d = blocks[k]
+
+        @pl.when(jnp.logical_not(jnp.logical_or(d == zl, jnp.logical_and(middle, d == far))))
         def _():
-            drain(TZ.at[k], s_dz + k)
+            drain(TZ.at[d], s_dz + k)
+
+    @pl.when(middle)
+    def _():
+        drain(TZ.at[far], s_dz + 4)
 
 
 def hand_over(a, b, d, a_out, b_out, d_out):
@@ -487,35 +528,37 @@
             shape((ROWS, D_ROW), BF16),
         ),
         in_specs=[vmem, anywhere, anywhere, anywhere],
-        out_specs=(vmem, vmem, vmem),
+        out_specs=(vmem, vmem, anywhere),
         scratch_shapes=[
             pltpu.VMEM((4, ROWS, WIN), BF16),
             pltpu.VMEM((2, 2, 4, 2, TOK, WIN), BF16),
             pltpu.VMEM((4, 4, 4, 64, ROWS), BF16),
             pltpu.VMEM((4, ROWS, 1024), BF16),
-            pltpu.VMEM((NC, 2, 2, 64, CW), BF16),
-            pltpu.VMEM((NC, 2, 2, 64, CW), BF16),
-            pltpu.VMEM((NC, 2, 2, 64, CW), BF16),
-            pltpu.VMEM((NC, 2, 2, 64, CW), BF16),
-            pltpu.VMEM((NC, 2, 2, 64, CW), BF16),
-            pltpu.VMEM((NC, 2, 2, 64, CW), BF16),
-            pltpu.VMEM((NC, 2, 2, 4, 64, CW), F32),
-            pltpu.VMEM((NC, 2, 2, TOK, CW), F32),
-            pltpu.VMEM((NC, 8, 16, CW), BF16),
-            pltpu.VMEM((NC, 8, 16, CW), BF16),
-            pltpu.VMEM((NC, 4, 16, CW), BF16),
-            pltpu.VMEM((NC, 4, 16, CW), BF16),
-            pltpu.VMEM((NC, TOK, CW), F32),
-            pltpu.VMEM((NC, TOK, CW), F32),
-            pltpu.VMEM((NC, TOK, CW), F32),
+            [pltpu.VMEM((2, 2, 64, w), BF16) for w in PW],
+            [pltpu.VMEM((2, 2, 64, w), BF16) for w in PW],
+            [pltpu.VMEM((2, 2, 64, w), BF16) for w in PW],
+            [pltpu.VMEM((2, 2, 64, w), BF16) for w in PW],
+            [pltpu.VMEM((2, 2, 64, w), BF16) for w in PW],
+            [pltpu.VMEM((2, 2, 64, w), BF16) for w in PW],
+            [pltpu.VMEM((4, 4, 64, w), F32) for w in PW],
+            [pltpu.VMEM((2, 2, TOK, w), F32) for w in PW],
+            [pltpu.VMEM((2, 2, TOK, w), BF16) for w in PW],
+            [pltpu.VMEM((2, 2, TOK, w), BF16) for w in PW],
+            [pltpu.VMEM((2, TOK, w), BF16) for w in PW],
+            [pltpu.VMEM((2, TOK, w), BF16) for w in PW],
+            [pltpu.VMEM((TOK, w), F32) for w in PW],
+            [pltpu.VMEM((TOK, w), F32) for w in PW],
+            [pltpu.VMEM((TOK, w), F32) for w in PW],
             pltpu.VMEM((4, 4, 2, 64, 256), BF16),
             pltpu.VMEM((4, 4, 2, 64, 256), BF16),
             pltpu.VMEM((4, 4, 2, 64, 256), BF16),
             pltpu.VMEM((4, 4, 2, 64, 256), BF16),
             pltpu.VMEM((4, 4, 2, 64, 256), BF16),
             pltpu.VMEM((4, 4, 2, 64, 256), BF16),
+            pltpu.VMEM((4, 2, 64, 256), BF16),
             pltpu.VMEM((3, NC, ROWS, CW), BF16),
             pltpu.VMEM((2, 2, NC, ROWS, CW), BF16),
+            pltpu.VMEM((ROWS, D_ROW), BF16),
             pltpu.SemaphoreType.DMA((N_SEMS,)),
             pltpu.SemaphoreType.DMA((N_SEMS,)),
             pltpu.SemaphoreType.DMA((16,)),

time: 109 us -> 107 us (0.982)
  the two profiles are of different devices: /device:TPU:45 before, /device:TPU:7 now
where the time goes in v3:
time: 107 us
  Pallas kernels  106 us (99%)
    pallas_call x1, Pallas kernels, per_device(): pl.pallas_call(kernel, out_shape=(shape((TOK, D_ROW), BF16), shape((64, 8...  103 us
    pallas_call x1, Pallas kernels, per_device(): pl.pallas_call(hand_over, out_shape=(shape((TOK, D_ROW), BF16), shape((64...  3.09 us

profile of v3, /device:TPU:7, one launch (start us, length us, event | category | flops | bytes accessed | tf_op | source)
XLA Modules:
  0.0 106.5 jit_solution(7027486849323748794)
XLA Ops:
  0.6 102.8 %shard_map.67 = (bf16[32,3712]{1,0:T(8,128)(2,1)}, bf16[64,1856]{1,0:T(8,128)(2,1)}, bf16[232,3712]{1,0:T(8,128)(2,1)}) custom-call(bf16[32,3712]{1,0:T(8,128)(2,1)} %res_ref.1, bf16[8,232,256]{2,1,0:T(8,128)(2,1)} %bitcast.7, bf16[232,3712]{1,0:T(8,128)(2,1)} %bitcast.5, bf16[32,3712]{1,0:T(8,128)(2,1)} %g_ref.1), custom_call_target="tpu_custom_call" | custom-call | flops 10947133440 | bytes 8388608 | tf_op jit(solution)/shard_map/pallas_call | solution.py:523
  103.4 3.1 %shard_map.68 = (bf16[32,3712]{1,0:T(8,128)(2,1)}, bf16[64,1856]{1,0:T(8,128)(2,1)}, bf16[232,3712]{1,0:T(8,128)(2,1)}) custom-call(bf16[32,3712]{1,0:T(8,128)(2,1)} %get-tuple-element.9.a, bf16[64,1856]{1,0:T(8,128)(2,1)} %get-tuple-element.10.b, bf16[232,3712]{1,0:T(8,128)(2,1)} %get-tuple-element.11.d), custom_call_target="tpu_custom_call" | custom-call | tf_op jit(solution)/shard_map/pallas_call | solution.py:573

commit v4 on v3

--- a/solution.py
+++ b/solution.py
@@ -30,7 +30,7 @@
         return base
 
 
-N_SEMS = 224
+S_SEMS, R_SEMS, L_SEMS = 69, 72, 8
 
 
 def kernel(
@@ -40,7 +40,7 @@
     bufA, RA, bufB1, bufB2, RB1, RB2, PF, accP,
     bufY, RY, bufZ, RZ, bufC, RC, own,
     OWN, DY, RDY, RDC, TZ, RDZ, RL,
-    DWs, RW, WG,
+    DWs, RW, WG, CG,
     ss, rs, ls,
 ):
     ia = lax.axis_index("ia")
@@ -117,16 +117,17 @@
     def window(cc):
         return pl.ds(pl.multiple_of(cc * SHIFT, 128), WIN)
 
-    r_g0 = r_idx.take(2)
-    r_g1 = r_idx.take(2)
+    r_g0 = r_idx.take(1)
+    r_g1 = r_idx.take(1)
     g_own = g_ref.at[:, window(c)]
     g_oth = g_ref.at[:, window(oc)]
     g_local = local(g_own, Gb.at[0, c, x, zh])
-    post(g_oth, Gb.at[0, c, x, zh], r_g0 + c, other_core)
-    post(g_own, Gb.at[0, c, x, zh], r_g1 + c, dev(hh=zn))
-    post(g_oth, Gb.at[0, c, x, zh], r_g1 + c, dev(hh=zn, cc=oc))
-
-    r_w = r_idx.take(4 * NC)
+    post(g_oth, Gb.at[0, c, x, zh], r_g0, other_core)
+    post(g_own, Gb.at[0, c, x, zh], r_g1, dev(hh=zn))
+    post(g_oth, Gb.at[0, c, x, zh], r_g1, dev(hh=zn, cc=oc))
+
+    r_w = r_idx.take(1 + NC)
+    s_w = s_idx.take(3)
 
     def w_cols(cc, j):
         return pl.ds(pl.multiple_of(cc * SHIFT + PO[j], 128), PW[j])
@@ -134,8 +135,8 @@
     def send_w(j):
         cols = pl.ds(PO[j], PW[j])
         for cc, yy in ((0, ya), (1, yb)):
-            post(w_ref.at[:, w_cols(cc, j)], Wb.at[2 + c, :, cols],
-                 r_w + (2 + c) * NC + j, dev(yy=yy, cc=cc))
+            send(w_ref.at[:, w_cols(cc, j)], Wb.at[2 + c, :, cols],
+                 r_w + 1 + j, dev(yy=yy, cc=cc), s_w + 1 + cc)
 
     r_y = r_idx.take(2)
     r_xp = r_idx.take(4)
@@ -164,7 +165,7 @@
         got(unit(1, x, h), r_y + k)
 
     g_local.wait()
-    got(Gb.at[0, oc, x, zh], r_g0 + oc)
+    got(Gb.at[0, oc, x, zh], r_g0)
     to_partner(0, zh)
     to_x(0, 0, zh)
 
@@ -196,7 +197,7 @@
     for j in range(NC):
         cols = pl.ds(PO[j], PW[j])
         w_locals.append(local(w_ref.at[:, w_cols(c, j)], Wb.at[c, :, cols]))
-        post(w_ref.at[:, w_cols(oc, j)], Wb.at[c, :, cols], r_w + c * NC + j, other_core)
+        send(w_ref.at[:, w_cols(oc, j)], Wb.at[c, :, cols], r_w, other_core, s_w)
 
 
     from_partner(0, zh)
@@ -218,8 +219,7 @@
             transpose_x(2 * half + sl, blk)
     forward_down(0, zh)
 
-    for core in range(2):
-        got(Gb.at[0, core, x, zn], r_g1 + core)
+    got(unit(0, x, zn), r_g1)
     to_partner(1, zn)
     to_x(0, 1, zn)
     send_w(1)
@@ -233,8 +233,7 @@
             transpose_x(2 * (1 - half) + sl, blk)
     for cp in w_locals:
         cp.wait()
-    for j in range(NC):
-        got(Wb.at[oc, :, pl.ds(PO[j], PW[j])], r_w + oc * NC + j)
+    got(Wb.at[oc], r_w)
 
     def project(j):
         @pl.loop(0, 4)
@@ -259,8 +258,7 @@
 
     def got_w(j):
         cols = pl.ds(PO[j], PW[j])
-        for s in (2, 3):
-            got(Wb.at[s, :, cols], r_w + s * NC + j)
+        got(Wb.at[2:4, :, cols], r_w + 1 + j)
         if j == 0:
             keep = (c == 0).astype(BF16)
             for s in range(4):
@@ -289,7 +287,8 @@
         bufB2[j][1] = (PF[j][2:4, xm] + RA[j][1].astype(F32)).astype(BF16)
         post(bufB2[j].at[1], RB2[j].at[1], r_b2 + 2 * j + 1, to_xm)
 
-    r_dy, r_dc, r_dz = r_idx.take(4), r_idx.take(16), r_idx.take(4)
+    r_dy, r_dc, r_dz = r_idx.take(4), r_idx.take(4), r_idx.take(4)
+    s_dc = s_idx.take(4)
     r_rl = r_idx.take(1)
     s_dz = s_idx.take(5)
     blocks = (x, xp, xm, x2)
@@ -310,8 +309,8 @@
         if last == 4:
             post(DY.at[k], RDY.at[k], r_dy + k, dev(yy=tp))
 
-    r_wg = r_idx.take(4 * NC)
-    s_wg = s_idx.take(3 * NC)
+    r_wg = r_idx.take(4)
+    s_wg = s_idx.take(3)
 
     def grad(s, j):
         cols = pl.ds(pl.multiple_of(j * CW, 128), CW)
@@ -325,13 +324,11 @@
         got(RDY.at[k], r_dy + k)
         for q in range(2):
             for part, group in ((OWN, own_groups[q]), (RDY, got_groups[q])):
-                post(part.at[k, pl.ds(2 * q, 2), oc], RDC.at[k, group],
-                     r_dc + 4 * k + group, other_core)
+                send(part.at[k, pl.ds(2 * q, 2), oc], RDC.at[k, group], r_dc + k, other_core, s_dc + k)
 
     def to_ao(k):
         d = blocks[k]
-        for group in range(4):
-            got(RDC.at[k, group], r_dc + 4 * k + group)
+        got(RDC.at[k], r_dc + k)
         for q in range(2):
             for part, group in ((OWN, own_groups[q]), (RDY, got_groups[q])):
                 TZ[d, group] = (part[k, 2 * q:2 * q + 2, c].astype(F32)
@@ -352,8 +349,8 @@
         def _():
             RDZ[zl] = TZ[d]
 
-    def relay_on():
-        @pl.when(middle)
+    def relay_on(when):
+        @pl.when(jnp.logical_and(middle, when))
         def _():
             got(RL, r_rl)
             TZ[far] = (TZ[far].astype(F32) + RL[...].astype(F32)).astype(BF16)
@@ -365,13 +362,13 @@
         @pl.loop(0, NC)
         def _(j):
             DWs[core, j] = grad(2 + core, j)
-            send(DWs.at[core, j], RW.at[c, 1, j], r_wg + (2 * c + 1) * NC + j, to, s_wg + core * NC + j)
+            send(DWs.at[core, j], RW.at[c, 1, j], r_wg + 2 * c + 1, to, s_wg + core)
 
     def grad_core():
         @pl.loop(0, NC)
         def _(j):
             DWs[2, j] = grad(oc, j)
-            send(DWs.at[2, j], RW.at[c, 0, j], r_wg + 2 * c * NC + j, other_core, s_wg + 2 * NC + j)
+            send(DWs.at[2, j], RW.at[c, 0, j], r_wg + 2 * c, other_core, s_wg + 2)
 
     def grad_own():
         @pl.loop(0, NC)
@@ -410,6 +407,7 @@
     pass_on(1)
     to_ao(2)
     to_core(3)
+    relay_on(jnp.logical_or(far == x, far == xp))
     grad_other(1)
     post_b(2)
     to_ao(3)
@@ -440,11 +438,9 @@
         post(bufC[j], RC[j], r_pc + j, other_core)
 
     def finish_weight_grad():
-        @pl.loop(0, NC)
-        def _(j):
-            got(RW.at[oc, 0, j], r_wg + 2 * oc * NC + j)
-            for w in range(2):
-                got(RW.at[w, 1, j], r_wg + (2 * w + 1) * NC + j)
+        got(RW.at[oc, 0], r_wg + 2 * oc)
+        for w in range(2):
+            got(RW.at[w, 1], r_wg + 2 * w + 1)
 
         for w in range(2):
             @pl.loop(0, NC)
@@ -466,12 +462,14 @@
         for m in (1, 2, 3):
             total = total + RDZ[m].astype(F32)
         total = total.astype(BF16).reshape(8, 64, 256)
-        cg_ref[...] = jnp.concatenate([total[g][:, :ROWS] for g in range(8)], axis=1)
+        CG[...] = jnp.concatenate([total[g][:, :ROWS] for g in range(8)], axis=1)
+        return local(CG, cg_ref)
 
     to_y(0)
     grad_core()
+    relay_on(far == xm)
     pass_on(2)
-    relay_on()
+    relay_on(far == x2)
     to_z(0)
     to_y(1)
     grad_own()
@@ -481,7 +479,7 @@
     wg_out = finish_weight_grad()
     to_c(0)
     to_c(1)
-    finish_context_grad()
+    cg_out = finish_context_grad()
     to_c(2)
 
     for j in range(NC):
@@ -493,11 +491,15 @@
             upd_ref[:, cols] = (res_ref[:, cols].astype(F32) + v).astype(BF16)
 
     wg_out.wait()
+    cg_out.wait()
     for cp in sent:
         cp.wait_send()
-    for j in range(NC):
-        for s in range(3):
-            drain(DWs.at[s, j], s_wg + s * NC + j)
+    for s in range(3):
+        drain(DWs.at[s], s_wg + s)
+    for k in range(4):
+        drain(RDC.at[k], s_dc + k)
+    for to in range(3):
+        drain(Wb.at[0], s_w + to)
     for k in range(4):
         d = blocks[k]
 
@@ -510,10 +512,19 @@
         drain(TZ.at[far], s_dz + 4)
 
 
-def hand_over(a, b, d, a_out, b_out, d_out):
-    a_out[...] = a[...]
-    b_out[...] = b[...]
-    d_out[...] = d[...]
+def hand_over(a, b, d, a_out, b_out, d_out, va, vb, vd, sems):
+    moves = [(d.at[:, pl.ds(o, n)], vd.at[:, pl.ds(o, n)], d_out.at[:, pl.ds(o, n)])
+             for o, n in ((0, 1024), (1024, 1024), (2048, 1024), (3072, 640))]
+    moves += [(a, va, a_out), (b, vb, b_out)]
+    arrive = [pltpu.make_async_copy(src, mid, sems.at[0, i]) for i, (src, mid, _) in enumerate(moves)]
+    leave = [pltpu.make_async_copy(mid, dst, sems.at[1, i]) for i, (_, mid, dst) in enumerate(moves)]
+    for cp in arrive:
+        cp.start()
+    for first, second in zip(arrive, leave):
+        first.wait()
+        second.start()
+    for cp in leave:
+        cp.wait()
 
 
 def per_device(residual, context, proj_weight, out_grad):
@@ -528,7 +539,7 @@
             shape((ROWS, D_ROW), BF16),
         ),
         in_specs=[vmem, anywhere, anywhere, anywhere],
-        out_specs=(vmem, vmem, anywhere),
+        out_specs=(vmem, anywhere, anywhere),
         scratch_shapes=[
             pltpu.VMEM((4, ROWS, WIN), BF16),
             pltpu.VMEM((2, 2, 4, 2, TOK, WIN), BF16),
@@ -559,9 +570,10 @@
             pltpu.VMEM((3, NC, ROWS, CW), BF16),
             pltpu.VMEM((2, 2, NC, ROWS, CW), BF16),
             pltpu.VMEM((ROWS, D_ROW), BF16),
-            pltpu.SemaphoreType.DMA((N_SEMS,)),
-            pltpu.SemaphoreType.DMA((N_SEMS,)),
-            pltpu.SemaphoreType.DMA((16,)),
+            pltpu.VMEM((64, 8 * ROWS), BF16),
+            pltpu.SemaphoreType.DMA((S_SEMS,)),
+            pltpu.SemaphoreType.DMA((R_SEMS,)),
+            pltpu.SemaphoreType.DMA((L_SEMS,)),
         ],
         compiler_params=pltpu.CompilerParams(
             collective_id=0, has_side_effects=True, vmem_limit_bytes=60 * 2**20
@@ -577,8 +589,14 @@
             shape((64, 8 * ROWS), BF16),
             shape((ROWS, D_ROW), BF16),
         ),
-        in_specs=[vmem] * 3,
-        out_specs=(vmem,) * 3,
+        in_specs=[anywhere] * 3,
+        out_specs=(anywhere,) * 3,
+        scratch_shapes=[
+            pltpu.VMEM((TOK, D_ROW), BF16),
+            pltpu.VMEM((64, 8 * ROWS), BF16),
+            pltpu.VMEM((ROWS, D_ROW), BF16),
+            pltpu.SemaphoreType.DMA((2, 6)),
+        ],
     )(updated, context_grad, weight_grad)
     return updated, context_grad, weight_grad[None]
 

time: 107 us -> 101 us (0.944)
  the two profiles are of different devices: /device:TPU:7 before, /device:TPU:97 now
where the time goes in v4:
time: 101 us; the launch traced here: 100 us
  Pallas kernels  99.8 us (99%)
    pallas_call x1, Pallas kernels, per_device(): pl.pallas_call(kernel, out_shape=(shape((TOK, D_ROW), BF16), shape((64, 8...  97.3 us
    pallas_call x1, Pallas kernels, per_device(): pl.pallas_call(hand_over, out_shape=(shape((TOK, D_ROW), BF16), shape((64...  2.47 us

profile of v4, /device:TPU:97, one launch (start us, length us, event | category | flops | bytes accessed | tf_op | source)
XLA Modules:
  0.0 100.4 jit_solution(3079407195233269284)
XLA Ops:
  0.6 97.3 %shard_map.67 = (bf16[32,3712]{1,0:T(8,128)(2,1)}, bf16[64,1856]{1,0:T(8,128)(2,1)}, bf16[232,3712]{1,0:T(8,128)(2,1)}) custom-call(bf16[32,3712]{1,0:T(8,128)(2,1)} %res_ref.1, bf16[8,232,256]{2,1,0:T(8,128)(2,1)} %bitcast.7, bf16[232,3712]{1,0:T(8,128)(2,1)} %bitcast.5, bf16[32,3712]{1,0:T(8,128)(2,1)} %g_ref.1), custom_call_target="tpu_custom_call" | custom-call | flops 10947133440 | bytes 8388608 | tf_op jit(solution)/shard_map/pallas_call | solution.py:534
  98.0 2.5 %shard_map.68 = (bf16[32,3712]{1,0:T(8,128)(2,1)}, bf16[64,1856]{1,0:T(8,128)(2,1)}, bf16[232,3712]{1,0:T(8,128)(2,1)}) custom-call(bf16[32,3712]{1,0:T(8,128)(2,1)} %get-tuple-element.9.a, bf16[64,1856]{1,0:T(8,128)(2,1)} %get-tuple-element.10.b, bf16[232,3712]{1,0:T(8,128)(2,1)} %get-tuple-element.11.d), custom_call_target="tpu_custom_call" | custom-call | tf_op jit(solution)/shard_map/pallas_call | solution.py:585

commit v5 on v4

--- a/solution.py
+++ b/solution.py
@@ -186,8 +186,10 @@
         t = XT[s, :, blk * 256:(blk + 1) * 256].T
         Xb[s, blk] = t.reshape(4, 64, ROWS)
 
-    for y_to, cc in ((yb, 0), (ya, 1)):
+    def send_context(y_to, cc):
         post(x_group(half, y_to, cc), x_block(half, 2 + c), r_c + 2 * (2 + c) + half, dev(yy=y_to, cc=cc))
+
+    send_context(tp, c)
     x_locals = []
     for q in range(2):
         x_locals.append(local(x_group(q, y, c), x_block(q, c)))
@@ -202,6 +204,7 @@
 
     from_partner(0, zh)
     to_x(1, 0, zh)
+    send_context(wp, oc)
     send_w(0)
     forward_up(0, zh)
     for cp in x_locals:
@@ -291,7 +294,9 @@
     s_dc = s_idx.take(4)
     r_rl = r_idx.take(1)
     s_dz = s_idx.take(5)
-    blocks = (x, xp, xm, x2)
+    edge = 2 * (1 - lax.min(x, 1))
+    n1, n2 = lax.rem(x + 1 + edge, 4), lax.rem(x + 3 + edge, 4)
+    blocks = (x, n1, n2, x2)
 
     def back(k, first=0, last=4):
         d = blocks[k]
@@ -381,14 +386,15 @@
     back(0, 0, 2)
     forward_down(1, zn)
     post_b(0)
-    project_chunk(1)
-    post_a(1)
+    got_w(1)
     got_w(2)
     back(0, 2, 4)
     for h, k in ((zh, 0), (zn, 1)):
         got(unit(1, xm, h), r_xp + 2 + k)
         got(unit(0, xp, h), r_xm + k)
     back(1)
+    project(1)
+    post_a(1)
     back(2)
     pass_on(0)
     post_b(1)
@@ -402,13 +408,13 @@
     grad_other(0)
     to_ao(1)
     to_core(2)
+    grad_other(1)
+    to_ao(2)
+    pass_on(1)
+    to_core(3)
+    relay_on(jnp.logical_or(far == x, far == n1))
     project(2)
     post_a(2)
-    pass_on(1)
-    to_ao(2)
-    to_core(3)
-    relay_on(jnp.logical_or(far == x, far == xp))
-    grad_other(1)
     post_b(2)
     to_ao(3)
 
@@ -467,16 +473,16 @@
 
     to_y(0)
     grad_core()
-    relay_on(far == xm)
+    relay_on(far == n2)
+    grad_own()
+    to_z(0)
+    relay_on(far == x2)
+    to_y(1)
     pass_on(2)
-    relay_on(far == x2)
-    to_z(0)
-    to_y(1)
-    grad_own()
+    to_z(1)
     to_y(2)
-    to_z(1)
+    wg_out = finish_weight_grad()
     to_z(2)
-    wg_out = finish_weight_grad()
     to_c(0)
     to_c(1)
     cg_out = finish_context_grad()

time: 101 us -> 98.5 us (0.975)
  the two profiles are of different devices: /device:TPU:97 before, /device:TPU:65 now
where the time goes in v5:
time: 98.5 us; the launch traced here: 96.7 us
  Pallas kernels  96.1 us (98%)
    pallas_call x1, Pallas kernels, per_device(): pl.pallas_call(kernel, out_shape=(shape((TOK, D_ROW), BF16), shape((64, 8...  93.6 us
    pallas_call x1, Pallas kernels, per_device(): pl.pallas_call(hand_over, out_shape=(shape((TOK, D_ROW), BF16), shape((64...  2.47 us

profile of v5, /device:TPU:65, one launch (start us, length us, event | category | flops | bytes accessed | tf_op | source)
XLA Modules:
  0.0 96.7 jit_solution(16969174246494790594)
XLA Ops:
  0.6 93.6 %shard_map.67 = (bf16[32,3712]{1,0:T(8,128)(2,1)}, bf16[64,1856]{1,0:T(8,128)(2,1)}, bf16[232,3712]{1,0:T(8,128)(2,1)}) custom-call(bf16[32,3712]{1,0:T(8,128)(2,1)} %res_ref.1, bf16[8,232,256]{2,1,0:T(8,128)(2,1)} %bitcast.7, bf16[232,3712]{1,0:T(8,128)(2,1)} %bitcast.5, bf16[32,3712]{1,0:T(8,128)(2,1)} %g_ref.1), custom_call_target="tpu_custom_call" | custom-call | flops 10947133440 | bytes 8388608 | tf_op jit(solution)/shard_map/pallas_call | solution.py:540
  94.3 2.5 %shard_map.68 = (bf16[32,3712]{1,0:T(8,128)(2,1)}, bf16[64,1856]{1,0:T(8,128)(2,1)}, bf16[232,3712]{1,0:T(8,128)(2,1)}) custom-call(bf16[32,3712]{1,0:T(8,128)(2,1)} %get-tuple-element.9.a, bf16[64,1856]{1,0:T(8,128)(2,1)} %get-tuple-element.10.b, bf16[232,3712]{1,0:T(8,128)(2,1)} %get-tuple-element.11.d), custom_call_target="tpu_custom_call" | custom-call | tf_op jit(solution)/shard_map/pallas_call | solution.py:591

commit v6 on v5

--- a/solution.py
+++ b/solution.py
@@ -15,8 +15,9 @@
 WIN = 1920
 NC = 3
 CW = WIN // NC
-PW = (768, 768, 384)
-PO = (0, 768, 1536)
+PW = (768, 512, 384, 256)
+PO = (0, 768, 1280, 1664)
+NP = len(PW)
 TOK = 32
 
 
@@ -30,7 +31,7 @@
         return base
 
 
-S_SEMS, R_SEMS, L_SEMS = 69, 72, 8
+S_SEMS, R_SEMS, L_SEMS = 83, 83, 9
 
 
 def kernel(
@@ -38,7 +39,7 @@
     upd_ref, cg_ref, wg_ref,
     Wb, Gb, Xb, XT,
     bufA, RA, bufB1, bufB2, RB1, RB2, PF, accP,
-    bufY, RY, bufZ, RZ, bufC, RC, own,
+    bufY, RY, bufZ, RZ, bufC, RC,
     OWN, DY, RDY, RDC, TZ, RDZ, RL,
     DWs, RW, WG, CG,
     ss, rs, ls,
@@ -78,9 +79,9 @@
     middle = lax.rem(zl, 3) != 0
     far = 3 * (1 - lax.rem(zl + 1, 2))
 
-    @pl.when(jnp.logical_not(middle))
-    def _():
-        RDZ[3 - zl] = jnp.zeros((4, 2, 64, 256), BF16)
+    mate = 3 - zl
+    absent = 3 * (1 - lax.div(zl, 2))
+    RDZ[absent] = jnp.zeros((4, 2, 64, 256), BF16)
 
     barrier = pltpu.get_barrier_semaphore()
     for p in partners:
@@ -126,7 +127,7 @@
     post(g_own, Gb.at[0, c, x, zh], r_g1, dev(hh=zn))
     post(g_oth, Gb.at[0, c, x, zh], r_g1, dev(hh=zn, cc=oc))
 
-    r_w = r_idx.take(1 + NC)
+    r_w = r_idx.take(1 + NP)
     s_w = s_idx.take(3)
 
     def w_cols(cc, j):
@@ -196,7 +197,7 @@
         post(x_group(q, y, oc), x_block(q, c), r_c + 2 * c + q, other_core)
 
     w_locals = []
-    for j in range(NC):
+    for j in range(NP):
         cols = pl.ds(PO[j], PW[j])
         w_locals.append(local(w_ref.at[:, w_cols(c, j)], Wb.at[c, :, cols]))
         send(w_ref.at[:, w_cols(oc, j)], Wb.at[c, :, cols], r_w, other_core, s_w)
@@ -225,8 +226,8 @@
     got(unit(0, x, zn), r_g1)
     to_partner(1, zn)
     to_x(0, 1, zn)
-    send_w(1)
-    send_w(2)
+    for j in range(1, NP):
+        send_w(j)
     from_partner(1, zn)
     to_x(1, 1, zn)
 
@@ -248,9 +249,9 @@
                 total = part if total is None else total + part
             PF[j][blk] = total.reshape(4, 64, PW[j])
 
-    r_a = r_idx.take(2 * NC)
-    r_b1 = r_idx.take(2 * NC)
-    r_b2 = r_idx.take(2 * NC)
+    r_a = r_idx.take(2 * NP)
+    r_b1 = r_idx.take(2 * NP)
+    r_b2 = r_idx.take(2 * NP)
     to_xp, to_xm = dev(xx=xp), dev(xx=xm)
 
     def drain(src, s):
@@ -292,10 +293,9 @@
 
     r_dy, r_dc, r_dz = r_idx.take(4), r_idx.take(4), r_idx.take(4)
     s_dc = s_idx.take(4)
-    r_rl = r_idx.take(1)
-    s_dz = s_idx.take(5)
-    edge = 2 * (1 - lax.min(x, 1))
-    n1, n2 = lax.rem(x + 1 + edge, 4), lax.rem(x + 3 + edge, 4)
+    r_rl = r_idx.take(2)
+    s_dz = s_idx.take(6)
+    n1, n2 = 3 - x, flip(x)
     blocks = (x, n1, n2, x2)
 
     def back(k, first=0, last=4):
@@ -339,12 +339,14 @@
                 TZ[d, group] = (part[k, 2 * q:2 * q + 2, c].astype(F32)
                                 + RDC[k, group].astype(F32)).astype(BF16)
 
-        relay = jnp.logical_and(jnp.logical_not(middle), d == 3 - zl)
-        held = jnp.logical_and(middle, d == far)
+        neighbour = 1 + lax.div(zl, 3)
+        relay = jnp.logical_and(jnp.logical_not(middle), jnp.logical_and(d != zl, d != neighbour))
+        held = jnp.logical_and(middle, jnp.logical_or(d == far, d == mate))
 
         @pl.when(relay)
         def _():
-            send(TZ.at[d], RL, r_rl, dev(ll=1 + lax.div(zl, 3)), s_dz + k)
+            r = lax.min(lax.rem(d, 3), 1)
+            send(TZ.at[d], RL.at[r], r_rl + r, dev(ll=neighbour), s_dz + k)
 
         @pl.when(jnp.logical_not(jnp.logical_or(relay, jnp.logical_or(held, d == zl))))
         def _():
@@ -354,12 +356,17 @@
         def _():
             RDZ[zl] = TZ[d]
 
-    def relay_on(when):
-        @pl.when(jnp.logical_and(middle, when))
-        def _():
-            got(RL, r_rl)
-            TZ[far] = (TZ[far].astype(F32) + RL[...].astype(F32)).astype(BF16)
-            send(TZ.at[far], RDZ.at[zl], r_dz + zl, dev(ll=far), s_dz + 4)
+    def relay_on(*ks):
+        for r, d in ((0, far), (1, mate)):
+            due = d == blocks[ks[0]]
+            for k in ks[1:]:
+                due = jnp.logical_or(due, d == blocks[k])
+
+            @pl.when(jnp.logical_and(middle, due))
+            def _():
+                got(RL.at[r], r_rl + r)
+                TZ[d] = (TZ[d].astype(F32) + RL[r].astype(F32)).astype(BF16)
+                send(TZ.at[d], RDZ.at[zl], r_dz + zl, dev(ll=d), s_dz + 4 + r)
 
     def grad_other(core):
         to = dev(yy=wp, cc=core)
@@ -379,6 +386,64 @@
         @pl.loop(0, NC)
         def _(j):
             RW[c, 0, j] = grad(c, j)
+
+    r_py, r_pz, r_pc = r_idx.take(NP), r_idx.take(NP), r_idx.take(NP)
+
+    def to_y(j):
+        got(RB1[j].at[1], r_b1 + 2 * j + 1)
+        got(RB2[j].at[1], r_b2 + 2 * j + 1)
+        v = PF[j][2:4, x] + RB1[j][1].astype(F32) + RB2[j][1].astype(F32)
+        bufY[j][...] = v.astype(BF16).reshape(2, 2, TOK, PW[j])
+        post(bufY[j], RY[j], r_py + j, dev(yy=tp))
+
+    def to_z(j):
+        got(RB1[j].at[0], r_b1 + 2 * j)
+        got(RB2[j].at[0], r_b2 + 2 * j)
+        v = PF[j][0:2, x] + RB1[j][0].astype(F32) + RB2[j][0].astype(F32)
+        got(RY[j], r_py + j)
+        v = v.reshape(2, 2, TOK, PW[j]) + RY[j][...].astype(F32)
+        accP[j][...] = v
+        bufZ[j][...] = accP[j][:, zn].astype(BF16)
+        post(bufZ[j].at[c], RZ[j].at[c], r_pz + j, dev(hh=zn))
+        post(bufZ[j].at[oc], RZ[j].at[c], r_pz + j, dev(hh=zn, cc=oc))
+        bufC[j][...] = accP[j][oc, zh]
+        post(bufC[j], RC[j], r_pc + j, other_core)
+
+    def finish_update(j):
+        got(RC[j], r_pc + j)
+        got(RZ[j], r_pz + j)
+        for w in (1, 0):
+            cols = slice(w * SHIFT + PO[j], w * SHIFT + PO[j] + PW[j])
+            v = jnp.where(c == w, accP[j][c, zh], RC[j][...]) + RZ[j][w].astype(F32)
+            upd_ref[:, cols] = (res_ref[:, cols].astype(F32) + v).astype(BF16)
+
+    def finish_weight_grad():
+        got(RW.at[oc, 0], r_wg + 2 * oc)
+        for w in range(2):
+            got(RW.at[w, 1], r_wg + 2 * w + 1)
+
+        for w in range(2):
+            @pl.loop(0, NC)
+            def _(j):
+                cols = pl.ds(pl.multiple_of(w * SHIFT + j * CW, 128), CW)
+                WG[:, cols] = (RW[w, 0, j].astype(F32) + RW[w, 1, j].astype(F32)).astype(BF16)
+
+        return local(WG, wg_ref)
+
+    def finish_context_grad():
+        for m in (1, 2, 3):
+            src = lax.rem(zl + m, 4)
+
+            @pl.when(src != absent)
+            def _():
+                got(RDZ.at[src], r_dz + src)
+
+        total = RDZ[0].astype(F32)
+        for m in (1, 2, 3):
+            total = total + RDZ[m].astype(F32)
+        total = total.astype(BF16).reshape(8, 64, 256)
+        CG[...] = jnp.concatenate([total[g][:, :ROWS] for g in range(8)], axis=1)
+        return local(CG, cg_ref)
 
     project_chunk(0)
     forward_up(1, zn)
@@ -386,8 +451,8 @@
     back(0, 0, 2)
     forward_down(1, zn)
     post_b(0)
-    got_w(1)
-    got_w(2)
+    for j in range(1, NP):
+        got_w(j)
     back(0, 2, 4)
     for h, k in ((zh, 0), (zn, 1)):
         got(unit(1, xm, h), r_xp + 2 + k)
@@ -412,89 +477,35 @@
     to_ao(2)
     pass_on(1)
     to_core(3)
-    relay_on(jnp.logical_or(far == x, far == n1))
+    relay_on(0, 1)
     project(2)
+    project(3)
     post_a(2)
+    post_a(3)
     post_b(2)
+    post_b(3)
+    to_y(0)
     to_ao(3)
 
-    r_py, r_pz, r_pc = r_idx.take(NC), r_idx.take(NC), r_idx.take(NC)
-
-    def to_y(j):
-        got(RB1[j].at[1], r_b1 + 2 * j + 1)
-        got(RB2[j].at[1], r_b2 + 2 * j + 1)
-        v = PF[j][2:4, x] + RB1[j][1].astype(F32) + RB2[j][1].astype(F32)
-        bufY[j][...] = v.astype(BF16).reshape(2, 2, TOK, PW[j])
-        post(bufY[j], RY[j], r_py + j, dev(yy=tp))
-
-    def to_z(j):
-        got(RB1[j].at[0], r_b1 + 2 * j)
-        got(RB2[j].at[0], r_b2 + 2 * j)
-        v = PF[j][0:2, x] + RB1[j][0].astype(F32) + RB2[j][0].astype(F32)
-        got(RY[j], r_py + j)
-        v = v.reshape(2, 2, TOK, PW[j]) + RY[j][...].astype(F32)
-        accP[j][...] = v
-        bufZ[j][...] = accP[j][:, zn].astype(BF16)
-        post(bufZ[j], RZ[j], r_pz + j, dev(hh=zn))
-
-    def to_c(j):
-        got(RZ[j], r_pz + j)
-        own[j][...] = accP[j][c, zh] + RZ[j][c].astype(F32)
-        bufC[j][...] = accP[j][oc, zh] + RZ[j][oc].astype(F32)
-        post(bufC[j], RC[j], r_pc + j, other_core)
-
-    def finish_weight_grad():
-        got(RW.at[oc, 0], r_wg + 2 * oc)
-        for w in range(2):
-            got(RW.at[w, 1], r_wg + 2 * w + 1)
-
-        for w in range(2):
-            @pl.loop(0, NC)
-            def _(j):
-                cols = pl.ds(pl.multiple_of(w * SHIFT + j * CW, 128), CW)
-                WG[:, cols] = (RW[w, 0, j].astype(F32) + RW[w, 1, j].astype(F32)).astype(BF16)
-
-        return local(WG, wg_ref)
-
-    def finish_context_grad():
-        for m in (1, 2, 3):
-            src = lax.rem(zl + m, 4)
-
-            @pl.when(jnp.logical_or(middle, src != 3 - zl))
-            def _():
-                got(RDZ.at[src], r_dz + src)
-
-        total = RDZ[0].astype(F32)
-        for m in (1, 2, 3):
-            total = total + RDZ[m].astype(F32)
-        total = total.astype(BF16).reshape(8, 64, 256)
-        CG[...] = jnp.concatenate([total[g][:, :ROWS] for g in range(8)], axis=1)
-        return local(CG, cg_ref)
-
-    to_y(0)
     grad_core()
-    relay_on(far == n2)
+    relay_on(2)
     grad_own()
     to_z(0)
-    relay_on(far == x2)
+    relay_on(3)
     to_y(1)
     pass_on(2)
+    pass_on(3)
     to_z(1)
     to_y(2)
+    to_y(3)
     wg_out = finish_weight_grad()
     to_z(2)
-    to_c(0)
-    to_c(1)
+    to_z(3)
+    finish_update(0)
+    finish_update(1)
     cg_out = finish_context_grad()
-    to_c(2)
-
-    for j in range(NC):
-        got(RC[j], r_pc + j)
-    for w in (1, 0):
-        for j in range(NC):
-            cols = slice(w * SHIFT + PO[j], w * SHIFT + PO[j] + PW[j])
-            v = jnp.where(c == w, own[j][...], RC[j][...])
-            upd_ref[:, cols] = (res_ref[:, cols].astype(F32) + v).astype(BF16)
+    finish_update(2)
+    finish_update(3)
 
     wg_out.wait()
     cg_out.wait()
@@ -509,13 +520,14 @@
     for k in range(4):
         d = blocks[k]
 
-        @pl.when(jnp.logical_not(jnp.logical_or(d == zl, jnp.logical_and(middle, d == far))))
+        @pl.when(jnp.logical_not(jnp.logical_or(d == zl, jnp.logical_and(middle, jnp.logical_or(d == far, d == mate)))))
         def _():
             drain(TZ.at[d], s_dz + k)
 
     @pl.when(middle)
     def _():
         drain(TZ.at[far], s_dz + 4)
+        drain(TZ.at[mate], s_dz + 5)
 
 
 def hand_over(a, b, d, a_out, b_out, d_out, va, vb, vd, sems):
@@ -565,14 +577,13 @@
             [pltpu.VMEM((2, TOK, w), BF16) for w in PW],
             [pltpu.VMEM((TOK, w), F32) for w in PW],
             [pltpu.VMEM((TOK, w), F32) for w in PW],
-            [pltpu.VMEM((TOK, w), F32) for w in PW],
             pltpu.VMEM((4, 4, 2, 64, 256), BF16),
             pltpu.VMEM((4, 4, 2, 64, 256), BF16),
             pltpu.VMEM((4, 4, 2, 64, 256), BF16),
             pltpu.VMEM((4, 4, 2, 64, 256), BF16),
             pltpu.VMEM((4, 4, 2, 64, 256), BF16),
             pltpu.VMEM((4, 4, 2, 64, 256), BF16),
-            pltpu.VMEM((4, 2, 64, 256), BF16),
+            pltpu.VMEM((2, 4, 2, 64, 256), BF16),
             pltpu.VMEM((3, NC, ROWS, CW), BF16),
             pltpu.VMEM((2, 2, NC, ROWS, CW), BF16),
             pltpu.VMEM((ROWS, D_ROW), BF16),

time: 98.5 us -> 97.4 us (0.989)
  the two profiles are of different devices: /device:TPU:65 before, /device:TPU:13 now
where the time goes in v6:
time: 97.4 us; the launch traced here: 97.3 us
  Pallas kernels  96.6 us (99%)
    pallas_call x1, Pallas kernels, per_device(): pl.pallas_call(kernel, out_shape=(shape((TOK, D_ROW), BF16), shape((64, 8...  94.2 us
    pallas_call x1, Pallas kernels, per_device(): pl.pallas_call(hand_over, out_shape=(shape((TOK, D_ROW), BF16), shape((64...  2.47 us

profile of v6, /device:TPU:13, one launch (start us, length us, event | category | flops | bytes accessed | tf_op | source)
XLA Modules:
  0.0 97.3 jit_solution(11438080488833460219)
XLA Ops:
  0.6 94.2 %shard_map.67 = (bf16[32,3712]{1,0:T(8,128)(2,1)}, bf16[64,1856]{1,0:T(8,128)(2,1)}, bf16[232,3712]{1,0:T(8,128)(2,1)}) custom-call(bf16[32,3712]{1,0:T(8,128)(2,1)} %res_ref.1, bf16[8,232,256]{2,1,0:T(8,128)(2,1)} %bitcast.7, bf16[232,3712]{1,0:T(8,128)(2,1)} %bitcast.5, bf16[32,3712]{1,0:T(8,128)(2,1)} %g_ref.1), custom_call_target="tpu_custom_call" | custom-call | flops 10947133440 | bytes 8388608 | tf_op jit(solution)/shard_map/pallas_call | solution.py:552
  94.8 2.5 %shard_map.68 = (bf16[32,3712]{1,0:T(8,128)(2,1)}, bf16[64,1856]{1,0:T(8,128)(2,1)}, bf16[232,3712]{1,0:T(8,128)(2,1)}) custom-call(bf16[32,3712]{1,0:T(8,128)(2,1)} %get-tuple-element.9.a, bf16[64,1856]{1,0:T(8,128)(2,1)} %get-tuple-element.10.b, bf16[232,3712]{1,0:T(8,128)(2,1)} %get-tuple-element.11.d), custom_call_target="tpu_custom_call" | custom-call | tf_op jit(solution)/shard_map/pallas_call | solution.py:602

commit v7 on v6

--- a/solution.py
+++ b/solution.py
@@ -13,6 +13,7 @@
 D_ROW = 3712
 SHIFT = 1792
 WIN = 1920
+SHARED = 128
 NC = 3
 CW = WIN // NC
 PW = (768, 512, 384, 256)
@@ -31,7 +32,7 @@
         return base
 
 
-S_SEMS, R_SEMS, L_SEMS = 83, 83, 9
+S_SEMS, R_SEMS, L_SEMS = 83, 84, 9
 
 
 def kernel(
@@ -83,6 +84,12 @@
     absent = 3 * (1 - lax.div(zl, 2))
     RDZ[absent] = jnp.zeros((4, 2, 64, 256), BF16)
 
+    @pl.when(c == 1)
+    def _():
+        Gb[:, :, :, :, :, 0:SHARED] = jnp.zeros((2, 2, 4, 2, TOK, SHARED), BF16)
+        Wb[2:4, :, 0:SHARED] = jnp.zeros((2, ROWS, SHARED), BF16)
+
+
     barrier = pltpu.get_barrier_semaphore()
     for p in partners:
         pl.semaphore_signal(barrier, inc=1, device_id=p, device_id_type=MESH)
@@ -90,6 +97,7 @@
 
     s_idx, r_idx, l_idx = Sems(), Sems(), Sems()
     sent = []
+    sent_cut = []
 
     def send(src, dst, r, to, s=None):
         if s is None:
@@ -104,6 +112,17 @@
     def post(*args):
         sent.append(send(*args))
 
+    def by_core(core, act):
+        for cc in range(2):
+            @pl.when(core == cc)
+            def _():
+                act(cc * SHARED)
+
+    def post_cut(core, src, dst, r, to):
+        i = s_idx.take(1)
+        by_core(core, lambda cut: send(src(cut), dst(cut), r, to, i))
+        sent_cut.append((core, src, i))
+
     def got(dst, r):
         pltpu.make_async_remote_copy(
             src_ref=dst, dst_ref=dst, send_sem=ss.at[0], recv_sem=rs.at[r],
@@ -115,17 +134,18 @@
         cp.start()
         return cp
 
-    def window(cc):
-        return pl.ds(pl.multiple_of(cc * SHIFT, 128), WIN)
-
     r_g0 = r_idx.take(1)
     r_g1 = r_idx.take(1)
-    g_own = g_ref.at[:, window(c)]
-    g_oth = g_ref.at[:, window(oc)]
-    g_local = local(g_own, Gb.at[0, c, x, zh])
-    post(g_oth, Gb.at[0, c, x, zh], r_g0, other_core)
-    post(g_own, Gb.at[0, c, x, zh], r_g1, dev(hh=zn))
-    post(g_oth, Gb.at[0, c, x, zh], r_g1, dev(hh=zn, cc=oc))
+    def g_part(cc):
+        return lambda cut: g_ref.at[:, pl.ds(pl.multiple_of(cc * SHIFT + cut, 128), WIN - cut)]
+
+    def g_slot(cut):
+        return Gb.at[0, c, x, zh, :, pl.ds(cut, WIN - cut)]
+
+    g_local = local(g_part(c)(0), Gb.at[0, c, x, zh])
+    post_cut(oc, g_part(oc), g_slot, r_g0, other_core)
+    post_cut(c, g_part(c), g_slot, r_g1, dev(hh=zn))
+    post_cut(oc, g_part(oc), g_slot, r_g1, dev(hh=zn, cc=oc))
 
     r_w = r_idx.take(1 + NP)
     s_w = s_idx.take(3)
@@ -134,10 +154,11 @@
         return pl.ds(pl.multiple_of(cc * SHIFT + PO[j], 128), PW[j])
 
     def send_w(j):
-        cols = pl.ds(PO[j], PW[j])
         for cc, yy in ((0, ya), (1, yb)):
-            send(w_ref.at[:, w_cols(cc, j)], Wb.at[2 + c, :, cols],
-                 r_w + 1 + j, dev(yy=yy, cc=cc), s_w + 1 + cc)
+            cut = cc * SHARED if j == 0 else 0
+            n = PW[j] - cut
+            src = w_ref.at[:, pl.ds(cc * SHIFT + PO[j] + cut, n)]
+            send(src, Wb.at[2 + c, :, pl.ds(PO[j] + cut, n)], r_w + 1 + j, dev(yy=yy, cc=cc), s_w + 1 + cc)
 
     r_y = r_idx.take(2)
     r_xp = r_idx.take(4)
@@ -145,28 +166,31 @@
     r_f = r_idx.take(4)
 
     def unit(p, xx, h):
-        return Gb.at[p, :, xx, h]
+        return lambda cut: Gb.at[p, :, xx, h, :, pl.ds(cut, WIN - cut)]
+
+    def got_unit(p, xx, h, r):
+        by_core(c, lambda cut: got(unit(p, xx, h)(cut), r))
 
     def to_x(p, k, h):
-        post(unit(p, x, h), unit(p, x, h), r_xp + 2 * p + k, dev(xx=xp))
-        post(unit(p, x, h), unit(p, x, h), r_xm + 2 * p + k, dev(xx=xm))
+        post_cut(c, unit(p, x, h), unit(p, x, h), r_xp + 2 * p + k, dev(xx=xp))
+        post_cut(c, unit(p, x, h), unit(p, x, h), r_xm + 2 * p + k, dev(xx=xm))
 
     def forward_up(k, h):
-        got(unit(0, xm, h), r_xp + k)
-        post(unit(0, xm, h), unit(0, xm, h), r_f + k, dev(xx=xp))
+        got_unit(0, xm, h, r_xp + k)
+        post_cut(c, unit(0, xm, h), unit(0, xm, h), r_f + k, dev(xx=xp))
 
     def forward_down(k, h):
-        got(unit(1, xp, h), r_xm + 2 + k)
-        post(unit(1, xp, h), unit(1, xp, h), r_f + 2 + k, dev(xx=xm))
+        got_unit(1, xp, h, r_xm + 2 + k)
+        post_cut(c, unit(1, xp, h), unit(1, xp, h), r_f + 2 + k, dev(xx=xm))
 
     def to_partner(k, h):
-        post(unit(0, x, h), unit(1, x, h), r_y + k, dev(yy=tp))
+        post_cut(c, unit(0, x, h), unit(1, x, h), r_y + k, dev(yy=tp))
 
     def from_partner(k, h):
-        got(unit(1, x, h), r_y + k)
+        got_unit(1, x, h, r_y + k)
 
     g_local.wait()
-    got(Gb.at[0, oc, x, zh], r_g0)
+    by_core(c, lambda cut: got(Gb.at[0, oc, x, zh, :, pl.ds(cut, WIN - cut)], r_g0))
     to_partner(0, zh)
     to_x(0, 0, zh)
 
@@ -223,7 +247,7 @@
             transpose_x(2 * half + sl, blk)
     forward_down(0, zh)
 
-    got(unit(0, x, zn), r_g1)
+    got_unit(0, x, zn, r_g1)
     to_partner(1, zn)
     to_x(0, 1, zn)
     for j in range(1, NP):
@@ -261,35 +285,53 @@
         ).wait_send()
 
     def got_w(j):
-        cols = pl.ds(PO[j], PW[j])
-        got(Wb.at[2:4, :, cols], r_w + 1 + j)
-        if j == 0:
-            keep = (c == 0).astype(BF16)
-            for s in range(4):
-                Wb[s, :, 0:128] = Wb[s, :, 0:128] * keep
+        if j > 0:
+            got(Wb.at[2:4, :, pl.ds(PO[j], PW[j])], r_w + 1 + j)
+            return
+        by_core(c, lambda cut: got(Wb.at[2:4, :, pl.ds(cut, PW[0] - cut)], r_w + 1))
+        keep = (c == 0).astype(BF16)
+        for s in range(2):
+            Wb[s, :, 0:SHARED] = Wb[s, :, 0:SHARED] * keep
 
     def project_chunk(j):
         got_w(j)
         project(j)
 
+    def part(ref, j, *where):
+        return lambda cut: ref[j].at[(*where, slice(None), slice(None), pl.ds(cut, PW[j] - cut))]
+
+    def post_part(j, src, dst, where, r, to):
+        a, b = part(src, j, *where), part(dst, j, *where)
+        if j == 0:
+            post_cut(c, a, b, r, to)
+        else:
+            post(a(0), b(0), r, to)
+
+    def got_part(j, dst, where, r):
+        a = part(dst, j, *where)
+        if j == 0:
+            by_core(c, lambda cut: got(a(cut), r))
+        else:
+            got(a(0), r)
+
     def post_a(j):
         bufA[j][...] = PF[j][:, x2].astype(BF16).reshape(2, 2, 64, PW[j])
-        post(bufA[j].at[0], RA[j].at[0], r_a + 2 * j, to_xp)
-        post(bufA[j].at[1], RA[j].at[1], r_a + 2 * j + 1, to_xm)
+        post_part(j, bufA, RA, (0,), r_a + 2 * j, to_xp)
+        post_part(j, bufA, RA, (1,), r_a + 2 * j + 1, to_xm)
 
     def post_b(j):
         bufB1[j][1] = PF[j][2:4, xp].astype(BF16)
-        post(bufB1[j].at[1], RB1[j].at[1], r_b1 + 2 * j + 1, to_xp)
+        post_part(j, bufB1, RB1, (1,), r_b1 + 2 * j + 1, to_xp)
         bufB2[j][0] = PF[j][0:2, xm].astype(BF16)
-        post(bufB2[j].at[0], RB2[j].at[0], r_b2 + 2 * j, to_xm)
+        post_part(j, bufB2, RB2, (0,), r_b2 + 2 * j, to_xm)
 
     def pass_on(j):
-        got(RA[j].at[0], r_a + 2 * j)
+        got_part(j, RA, (0,), r_a + 2 * j)
         bufB1[j][0] = (PF[j][0:2, xp] + RA[j][0].astype(F32)).astype(BF16)
-        post(bufB1[j].at[0], RB1[j].at[0], r_b1 + 2 * j, to_xp)
-        got(RA[j].at[1], r_a + 2 * j + 1)
+        post_part(j, bufB1, RB1, (0,), r_b1 + 2 * j, to_xp)
+        got_part(j, RA, (1,), r_a + 2 * j + 1)
         bufB2[j][1] = (PF[j][2:4, xm] + RA[j][1].astype(F32)).astype(BF16)
-        post(bufB2[j].at[1], RB2[j].at[1], r_b2 + 2 * j + 1, to_xm)
+        post_part(j, bufB2, RB2, (1,), r_b2 + 2 * j + 1, to_xm)
 
     r_dy, r_dc, r_dz = r_idx.take(4), r_idx.take(4), r_idx.take(4)
     s_dc = s_idx.take(4)
@@ -387,31 +429,44 @@
         def _(j):
             RW[c, 0, j] = grad(c, j)
 
-    r_py, r_pz, r_pc = r_idx.take(NP), r_idx.take(NP), r_idx.take(NP)
+    r_py, r_pz, r_pc = r_idx.take(NP), r_idx.take(NP + 1), r_idx.take(NP)
 
     def to_y(j):
-        got(RB1[j].at[1], r_b1 + 2 * j + 1)
-        got(RB2[j].at[1], r_b2 + 2 * j + 1)
+        got_part(j, RB1, (1,), r_b1 + 2 * j + 1)
+        got_part(j, RB2, (1,), r_b2 + 2 * j + 1)
         v = PF[j][2:4, x] + RB1[j][1].astype(F32) + RB2[j][1].astype(F32)
         bufY[j][...] = v.astype(BF16).reshape(2, 2, TOK, PW[j])
-        post(bufY[j], RY[j], r_py + j, dev(yy=tp))
+        post_part(j, bufY, RY, (slice(None),), r_py + j, dev(yy=tp))
+
+    def post_z(j, core):
+        def rows(ref, i):
+            return lambda cut: ref[j].at[i, :, pl.ds(cut, PW[j] - cut)]
+
+        if j == 0:
+            post_cut(c, rows(bufZ, core), rows(RZ, c), r_pz + NP * c, dev(hh=zn, cc=core))
+        else:
+            post(bufZ[j].at[core], RZ[j].at[c], r_pz + j, dev(hh=zn, cc=core))
 
     def to_z(j):
-        got(RB1[j].at[0], r_b1 + 2 * j)
-        got(RB2[j].at[0], r_b2 + 2 * j)
+        got_part(j, RB1, (0,), r_b1 + 2 * j)
+        got_part(j, RB2, (0,), r_b2 + 2 * j)
         v = PF[j][0:2, x] + RB1[j][0].astype(F32) + RB2[j][0].astype(F32)
-        got(RY[j], r_py + j)
+        got_part(j, RY, (slice(None),), r_py + j)
         v = v.reshape(2, 2, TOK, PW[j]) + RY[j][...].astype(F32)
         accP[j][...] = v
         bufZ[j][...] = accP[j][:, zn].astype(BF16)
-        post(bufZ[j].at[c], RZ[j].at[c], r_pz + j, dev(hh=zn))
-        post(bufZ[j].at[oc], RZ[j].at[c], r_pz + j, dev(hh=zn, cc=oc))
+        for core in (c, oc):
+            post_z(j, core)
         bufC[j][...] = accP[j][oc, zh]
         post(bufC[j], RC[j], r_pc + j, other_core)
 
     def finish_update(j):
         got(RC[j], r_pc + j)
-        got(RZ[j], r_pz + j)
+        if j == 0:
+            got(RZ[0].at[0], r_pz)
+            got(RZ[0].at[1, :, pl.ds(SHARED, PW[0] - SHARED)], r_pz + NP)
+        else:
+            got(RZ[j], r_pz + j)
         for w in (1, 0):
             cols = slice(w * SHIFT + PO[j], w * SHIFT + PO[j] + PW[j])
             v = jnp.where(c == w, accP[j][c, zh], RC[j][...]) + RZ[j][w].astype(F32)
@@ -422,7 +477,7 @@
         for w in range(2):
             got(RW.at[w, 1], r_wg + 2 * w + 1)
 
-        for w in range(2):
+        for w in (1, 0):
             @pl.loop(0, NC)
             def _(j):
                 cols = pl.ds(pl.multiple_of(w * SHIFT + j * CW, 128), CW)
@@ -455,8 +510,8 @@
         got_w(j)
     back(0, 2, 4)
     for h, k in ((zh, 0), (zn, 1)):
-        got(unit(1, xm, h), r_xp + 2 + k)
-        got(unit(0, xp, h), r_xm + k)
+        got_unit(1, xm, h, r_xp + 2 + k)
+        got_unit(0, xp, h, r_xm + k)
     back(1)
     project(1)
     post_a(1)
@@ -465,8 +520,8 @@
     post_b(1)
     to_core(0)
     for k, h in ((0, zh), (1, zn)):
-        got(unit(0, x2, h), r_f + k)
-        got(unit(1, x2, h), r_f + 2 + k)
+        got_unit(0, x2, h, r_f + k)
+        got_unit(1, x2, h, r_f + 2 + k)
     back(3)
     to_ao(0)
     to_core(1)
@@ -511,12 +566,18 @@
     cg_out.wait()
     for cp in sent:
         cp.wait_send()
+    for cc in range(2):
+        for core, src, i in sent_cut:
+            @pl.when(core == cc)
+            def _():
+                drain(src(cc * SHARED), i)
+
     for s in range(3):
         drain(DWs.at[s], s_wg + s)
     for k in range(4):
         drain(RDC.at[k], s_dc + k)
-    for to in range(3):
-        drain(Wb.at[0], s_w + to)
+    for to, n in ((0, WIN), (1, WIN), (2, WIN - SHARED)):
+        drain(Wb.at[0, :, pl.ds(0, n)], s_w + to)
     for k in range(4):
         d = blocks[k]
 

time: 97.4 us -> 95.2 us (0.977)
  the two profiles are of different devices: /device:TPU:13 before, /device:TPU:65 now
where the time goes in v7:
time: 95.2 us; the launch traced here: 94.3 us
  Pallas kernels  93.7 us (98%)
    pallas_call x1, Pallas kernels, per_device(): pl.pallas_call(kernel, out_shape=(shape((TOK, D_ROW), BF16), shape((64, 8...  91.2 us
    pallas_call x1, Pallas kernels, per_device(): pl.pallas_call(hand_over, out_shape=(shape((TOK, D_ROW), BF16), shape((64...  2.47 us

profile of v7, /device:TPU:65, one launch (start us, length us, event | category | flops | bytes accessed | tf_op | source)
XLA Modules:
  0.0 94.3 jit_solution(5977237793172379718)
XLA Ops:
  0.6 91.2 %shard_map.67 = (bf16[32,3712]{1,0:T(8,128)(2,1)}, bf16[64,1856]{1,0:T(8,128)(2,1)}, bf16[232,3712]{1,0:T(8,128)(2,1)}) custom-call(bf16[32,3712]{1,0:T(8,128)(2,1)} %res_ref.1, bf16[8,232,256]{2,1,0:T(8,128)(2,1)} %bitcast.7, bf16[232,3712]{1,0:T(8,128)(2,1)} %bitcast.5, bf16[32,3712]{1,0:T(8,128)(2,1)} %g_ref.1), custom_call_target="tpu_custom_call" | custom-call | flops 10947133440 | bytes 8388608 | tf_op jit(solution)/shard_map/pallas_call | solution.py:613
  91.9 2.5 %shard_map.68 = (bf16[32,3712]{1,0:T(8,128)(2,1)}, bf16[64,1856]{1,0:T(8,128)(2,1)}, bf16[232,3712]{1,0:T(8,128)(2,1)}) custom-call(bf16[32,3712]{1,0:T(8,128)(2,1)} %get-tuple-element.9.a, bf16[64,1856]{1,0:T(8,128)(2,1)} %get-tuple-element.10.b, bf16[232,3712]{1,0:T(8,128)(2,1)} %get-tuple-element.11.d), custom_call_target="tpu_custom_call" | custom-call | tf_op jit(solution)/shard_map/pallas_call | solution.py:663

commit v8 on v7

--- a/solution.py
+++ b/solution.py
@@ -545,17 +545,17 @@
     grad_core()
     relay_on(2)
     grad_own()
+    relay_on(3)
     to_z(0)
-    relay_on(3)
     to_y(1)
     pass_on(2)
     pass_on(3)
-    to_z(1)
     to_y(2)
     to_y(3)
-    wg_out = finish_weight_grad()
+    to_z(1)
     to_z(2)
     to_z(3)
+    wg_out = finish_weight_grad()
     finish_update(0)
     finish_update(1)
     cg_out = finish_context_grad()

time: 95.2 us -> 95.2 us (level)
  no operation moved by 1% of the time
where the time goes in v8:
time: 95.2 us; the launch traced here: 95.1 us
  Pallas kernels  94.4 us (99%)
    pallas_call x1, Pallas kernels, per_device(): pl.pallas_call(kernel, out_shape=(shape((TOK, D_ROW), BF16), shape((64, 8...  91.9 us
    pallas_call x1, Pallas kernels, per_device(): pl.pallas_call(hand_over, out_shape=(shape((TOK, D_ROW), BF16), shape((64...  2.47 us

profile of v8, /device:TPU:65, one launch (start us, length us, event | category | flops | bytes accessed | tf_op | source)
XLA Modules:
  0.0 95.1 jit_solution(1941183712554998312)
XLA Ops:
  0.6 91.9 %shard_map.67 = (bf16[32,3712]{1,0:T(8,128)(2,1)}, bf16[64,1856]{1,0:T(8,128)(2,1)}, bf16[232,3712]{1,0:T(8,128)(2,1)}) custom-call(bf16[32,3712]{1,0:T(8,128)(2,1)} %res_ref.1, bf16[8,232,256]{2,1,0:T(8,128)(2,1)} %bitcast.7, bf16[232,3712]{1,0:T(8,128)(2,1)} %bitcast.5, bf16[32,3712]{1,0:T(8,128)(2,1)} %g_ref.1), custom_call_target="tpu_custom_call" | custom-call | flops 10947133440 | bytes 8388608 | tf_op jit(solution)/shard_map/pallas_call | solution.py:613
  92.6 2.5 %shard_map.68 = (bf16[32,3712]{1,0:T(8,128)(2,1)}, bf16[64,1856]{1,0:T(8,128)(2,1)}, bf16[232,3712]{1,0:T(8,128)(2,1)}) custom-call(bf16[32,3712]{1,0:T(8,128)(2,1)} %get-tuple-element.9.a, bf16[64,1856]{1,0:T(8,128)(2,1)} %get-tuple-element.10.b, bf16[232,3712]{1,0:T(8,128)(2,1)} %get-tuple-element.11.d), custom_call_target="tpu_custom_call" | custom-call | tf_op jit(solution)/shard_map/pallas_call | solution.py:663

commit v9 on v8

--- a/solution.py
+++ b/solution.py
@@ -32,7 +32,7 @@
         return base
 
 
-S_SEMS, R_SEMS, L_SEMS = 83, 84, 9
+S_SEMS, R_SEMS, L_SEMS = 66, 84, 9
 
 
 def kernel(
@@ -118,10 +118,11 @@
             def _():
                 act(cc * SHARED)
 
-    def post_cut(core, src, dst, r, to):
-        i = s_idx.take(1)
+    def post_cut(core, src, dst, r, to, group=None):
+        i = s_idx.take(1) if group is None else group
         by_core(core, lambda cut: send(src(cut), dst(cut), r, to, i))
-        sent_cut.append((core, src, i))
+        if group is None:
+            sent_cut.append((core, src, i))
 
     def got(dst, r):
         pltpu.make_async_remote_copy(
@@ -165,6 +166,8 @@
     r_xm = r_idx.take(4)
     r_f = r_idx.take(4)
 
+    s_x, s_f, s_y = s_idx.take(1), s_idx.take(1), s_idx.take(1)
+
     def unit(p, xx, h):
         return lambda cut: Gb.at[p, :, xx, h, :, pl.ds(cut, WIN - cut)]
 
@@ -172,19 +175,19 @@
         by_core(c, lambda cut: got(unit(p, xx, h)(cut), r))
 
     def to_x(p, k, h):
-        post_cut(c, unit(p, x, h), unit(p, x, h), r_xp + 2 * p + k, dev(xx=xp))
-        post_cut(c, unit(p, x, h), unit(p, x, h), r_xm + 2 * p + k, dev(xx=xm))
+        post_cut(c, unit(p, x, h), unit(p, x, h), r_xp + 2 * p + k, dev(xx=xp), s_x)
+        post_cut(c, unit(p, x, h), unit(p, x, h), r_xm + 2 * p + k, dev(xx=xm), s_x)
 
     def forward_up(k, h):
         got_unit(0, xm, h, r_xp + k)
-        post_cut(c, unit(0, xm, h), unit(0, xm, h), r_f + k, dev(xx=xp))
+        post_cut(c, unit(0, xm, h), unit(0, xm, h), r_f + k, dev(xx=xp), s_f)
 
     def forward_down(k, h):
         got_unit(1, xp, h, r_xm + 2 + k)
-        post_cut(c, unit(1, xp, h), unit(1, xp, h), r_f + 2 + k, dev(xx=xm))
+        post_cut(c, unit(1, xp, h), unit(1, xp, h), r_f + 2 + k, dev(xx=xm), s_f)
 
     def to_partner(k, h):
-        post_cut(c, unit(0, x, h), unit(1, x, h), r_y + k, dev(yy=tp))
+        post_cut(c, unit(0, x, h), unit(1, x, h), r_y + k, dev(yy=tp), s_y)
 
     def from_partner(k, h):
         got_unit(1, x, h, r_y + k)
@@ -334,7 +337,7 @@
         post_part(j, bufB2, RB2, (1,), r_b2 + 2 * j + 1, to_xm)
 
     r_dy, r_dc, r_dz = r_idx.take(4), r_idx.take(4), r_idx.take(4)
-    s_dc = s_idx.take(4)
+    s_dc, s_dy = s_idx.take(1), s_idx.take(1)
     r_rl = r_idx.take(2)
     s_dz = s_idx.take(6)
     n1, n2 = 3 - x, flip(x)
@@ -354,7 +357,7 @@
             DY[k, s] = t[1]
 
         if last == 4:
-            post(DY.at[k], RDY.at[k], r_dy + k, dev(yy=tp))
+            send(DY.at[k], RDY.at[k], r_dy + k, dev(yy=tp), s_dy)
 
     r_wg = r_idx.take(4)
     s_wg = s_idx.take(3)
@@ -371,7 +374,7 @@
         got(RDY.at[k], r_dy + k)
         for q in range(2):
             for part, group in ((OWN, own_groups[q]), (RDY, got_groups[q])):
-                send(part.at[k, pl.ds(2 * q, 2), oc], RDC.at[k, group], r_dc + k, other_core, s_dc + k)
+                send(part.at[k, pl.ds(2 * q, 2), oc], RDC.at[k, group], r_dc + k, other_core, s_dc)
 
     def to_ao(k):
         d = blocks[k]
@@ -566,6 +569,9 @@
     cg_out.wait()
     for cp in sent:
         cp.wait_send()
+    sent_cut.append((c, lambda cut: Gb.at[:, :, 0:2, :, :, pl.ds(cut, WIN - cut)], s_x))
+    sent_cut.append((c, lambda cut: Gb.at[:, :, 0, :, :, pl.ds(cut, WIN - cut)], s_f))
+    sent_cut.append((c, lambda cut: Gb.at[0, :, 0, :, :, pl.ds(cut, WIN - cut)], s_y))
     for cc in range(2):
         for core, src, i in sent_cut:
             @pl.when(core == cc)
@@ -574,8 +580,8 @@
 
     for s in range(3):
         drain(DWs.at[s], s_wg + s)
-    for k in range(4):
-        drain(RDC.at[k], s_dc + k)
+    drain(RDC, s_dc)
+    drain(DY, s_dy)
     for to, n in ((0, WIN), (1, WIN), (2, WIN - SHARED)):
         drain(Wb.at[0, :, pl.ds(0, n)], s_w + to)
     for k in range(4):

time: 95.2 us -> 95 us (level)
  no operation moved by 1% of the time
where the time goes in v9:
time: 95 us; the launch traced here: 94.9 us
  Pallas kernels  94.2 us (99%)
    pallas_call x1, Pallas kernels, per_device(): pl.pallas_call(kernel, out_shape=(shape((TOK, D_ROW), BF16), shape((64, 8...  91.8 us
    pallas_call x1, Pallas kernels, per_device(): pl.pallas_call(hand_over, out_shape=(shape((TOK, D_ROW), BF16), shape((64...  2.47 us

profile of v9, /device:TPU:65, one launch (start us, length us, event | category | flops | bytes accessed | tf_op | source)
XLA Modules:
  0.0 94.9 jit_solution(3728674819135894175)
XLA Ops:
  0.6 91.8 %shard_map.67 = (bf16[32,3712]{1,0:T(8,128)(2,1)}, bf16[64,1856]{1,0:T(8,128)(2,1)}, bf16[232,3712]{1,0:T(8,128)(2,1)}) custom-call(bf16[32,3712]{1,0:T(8,128)(2,1)} %res_ref.1, bf16[8,232,256]{2,1,0:T(8,128)(2,1)} %bitcast.7, bf16[232,3712]{1,0:T(8,128)(2,1)} %bitcast.5, bf16[32,3712]{1,0:T(8,128)(2,1)} %g_ref.1), custom_call_target="tpu_custom_call" | custom-call | flops 10947133440 | bytes 8388608 | tf_op jit(solution)/shard_map/pallas_call | solution.py:619
  92.4 2.5 %shard_map.68 = (bf16[32,3712]{1,0:T(8,128)(2,1)}, bf16[64,1856]{1,0:T(8,128)(2,1)}, bf16[232,3712]{1,0:T(8,128)(2,1)}) custom-call(bf16[32,3712]{1,0:T(8,128)(2,1)} %get-tuple-element.9.a, bf16[64,1856]{1,0:T(8,128)(2,1)} %get-tuple-element.10.b, bf16[232,3712]{1,0:T(8,128)(2,1)} %get-tuple-element.11.d), custom_call_target="tpu_custom_call" | custom-call | tf_op jit(solution)/shard_map/pallas_call | solution.py:669

commit v10 on v8

--- a/solution.py
+++ b/solution.py
@@ -534,13 +534,13 @@
     to_core(3)
     relay_on(0, 1)
     project(2)
+    to_ao(3)
     project(3)
     post_a(2)
     post_a(3)
     post_b(2)
     post_b(3)
     to_y(0)
-    to_ao(3)
 
     grad_core()
     relay_on(2)
@@ -593,7 +593,7 @@
 
 def hand_over(a, b, d, a_out, b_out, d_out, va, vb, vd, sems):
     moves = [(d.at[:, pl.ds(o, n)], vd.at[:, pl.ds(o, n)], d_out.at[:, pl.ds(o, n)])
-             for o, n in ((0, 1024), (1024, 1024), (2048, 1024), (3072, 640))]
+             for o, n in ((0, 768), (768, 768), (1536, 768), (2304, 768), (3072, 384), (3456, 256))]
     moves += [(a, va, a_out), (b, vb, b_out)]
     arrive = [pltpu.make_async_copy(src, mid, sems.at[0, i]) for i, (src, mid, _) in enumerate(moves)]
     leave = [pltpu.make_async_copy(mid, dst, sems.at[1, i]) for i, (_, mid, dst) in enumerate(moves)]
@@ -673,7 +673,7 @@
             pltpu.VMEM((TOK, D_ROW), BF16),
             pltpu.VMEM((64, 8 * ROWS), BF16),
             pltpu.VMEM((ROWS, D_ROW), BF16),
-            pltpu.SemaphoreType.DMA((2, 6)),
+            pltpu.SemaphoreType.DMA((2, 8)),
         ],
     )(updated, context_grad, weight_grad)
     return updated, context_grad, weight_grad[None]

time: 95.2 us -> 95.2 us (level)
  no operation moved by 1% of the time
where the time goes in v10:
time: 95.2 us; the launch traced here: 95 us
  Pallas kernels  94.4 us (99%)
    pallas_call x1, Pallas kernels, per_device(): pl.pallas_call(kernel, out_shape=(shape((TOK, D_ROW), BF16), shape((64, 8...  91.9 us
    pallas_call x1, Pallas kernels, per_device(): pl.pallas_call(hand_over, out_shape=(shape((TOK, D_ROW), BF16), shape((64...  2.46 us

profile of v10, /device:TPU:65, one launch (start us, length us, event | category | flops | bytes accessed | tf_op | source)
XLA Modules:
  0.0 95.0 jit_solution(12265597982819438246)
XLA Ops:
  0.6 91.9 %shard_map.67 = (bf16[32,3712]{1,0:T(8,128)(2,1)}, bf16[64,1856]{1,0:T(8,128)(2,1)}, bf16[232,3712]{1,0:T(8,128)(2,1)}) custom-call(bf16[32,3712]{1,0:T(8,128)(2,1)} %res_ref.1, bf16[8,232,256]{2,1,0:T(8,128)(2,1)} %bitcast.7, bf16[232,3712]{1,0:T(8,128)(2,1)} %bitcast.5, bf16[32,3712]{1,0:T(8,128)(2,1)} %g_ref.1), custom_call_target="tpu_custom_call" | custom-call | flops 10947133440 | bytes 8388608 | tf_op jit(solution)/shard_map/pallas_call | solution.py:613
  92.6 2.5 %shard_map.68 = (bf16[32,3712]{1,0:T(8,128)(2,1)}, bf16[64,1856]{1,0:T(8,128)(2,1)}, bf16[232,3712]{1,0:T(8,128)(2,1)}) custom-call(bf16[32,3712]{1,0:T(8,128)(2,1)} %get-tuple-element.9.a, bf16[64,1856]{1,0:T(8,128)(2,1)} %get-tuple-element.10.b, bf16[232,3712]{1,0:T(8,128)(2,1)} %get-tuple-element.11.d), custom_call_target="tpu_custom_call" | custom-call | tf_op jit(solution)/shard_map/pallas_call | solution.py:663
